TPU v7x, 256 devices: a whole 4x4x8 slice. The times are simulated.
256 devices in a mesh: row: 32 (over z_hi, y, core), col: 8 (over z_lo, x).
Axes of the slice: x: 4, y: 4, z: 8 (z_hi: 4, z_lo: 2; z = z_hi * 2 + z_lo), core: 2. Of those that a mesh axis runs over, the one named last changes fastest.
Arguments:
- clips: bfloat16 [20480, 1024], P(('row', 'col')), may hold values from -8 to 8
- labels: int32 [20480], P(('row', 'col')), may hold values from 0 to 1023
Outputs:
- distances: float32 [20480, 1024], P(('row', 'col'))
All inputs are finite; a program needn't handle non-finite values.
Results may differ from a plain program's by a relative error of at most 0.002.
Values may be sent and summed in bfloat16 or wider, within the bound.
No kernel may reach another device: no remote copies, remote signals or barrier semaphores. Data moves between devices by JAX's collectives and lax.ppermute only.
A program may use at most 64 MiB of HBM per device.

v0:
```python
import functools

import jax
import jax.numpy as jnp
from jax import lax
from jax.experimental import pallas as pl
from jax.experimental.pallas import tpu as pltpu
from jax.sharding import Mesh, PartitionSpec as P

D = 1024
CLUSTERS = 1024
META = 128
WIDE = D + META
ROWS = 80
LOG2E = 1.4426950408889634
SCALE = LOG2E / D
F32 = jnp.float32
BF16 = jnp.bfloat16
TRANSPOSED = (((1,), (1,)), ((), ()))
AXES = ("z_hi", "y", "core", "z_lo", "x")
SIZES = (4, 4, 2, 2, 4)
Z = ("z_hi", "z_lo")
PLANE = ("y", "core", "x")


def call(body, outs, cost, *args):
    flops, size = 0, 0
    return pl.pallas_call(
        body,
        out_shape=outs,
        compiler_params=pltpu.CompilerParams(vmem_limit_bytes=40 * 2**20),
        cost_estimate=pl.CostEstimate(flops=flops, bytes_accessed=size, transcendentals=0),
    )(*args)


def shape(dims, dtype):
    return jax.ShapeDtypeStruct(dims, dtype)


def pack_kernel(clips_ref, labels_ref, out_ref):
    x = clips_ref[...]
    wide = x.astype(F32)
    half = jnp.sum(wide * wide, axis=1, keepdims=True) * (0.5 * SCALE)
    row = lax.broadcasted_iota(jnp.int32, (ROWS, ROWS), 0)
    col = lax.broadcasted_iota(jnp.int32, (ROWS, ROWS), 1)
    same = row == col
    label = jnp.sum(jnp.where(same, labels_ref[...].astype(F32), 0.0), axis=1, keepdims=True)
    half_row = jnp.sum(jnp.where(same, half, 0.0), axis=0, keepdims=True)
    gram = lax.dot_general(x, x, TRANSPOSED, preferred_element_type=F32)
    near = jnp.exp2(gram * SCALE - half - half_row)
    offset = jnp.sum(jnp.where(same, 0.0, near), axis=1, keepdims=True) * (1.0 / (ROWS - 1))
    first = half.astype(BF16).astype(F32)
    second = (half - first).astype(BF16).astype(F32)
    third = half - first - second
    upper = jnp.floor(label * (1.0 / 32.0))
    lower = label - 32.0 * upper
    lane = lax.broadcasted_iota(jnp.int32, (ROWS, META), 1)
    meta = jnp.zeros((ROWS, META), F32)
    for place, value in enumerate((first, second, third, upper, lower, offset)):
        meta = jnp.where(lane == place, value, meta)
    out_ref[:, :D] = x
    out_ref[:, D:] = meta.astype(BF16)


def split_meta(meta):
    wide = meta.astype(F32)
    half = wide[:, 0:1] + wide[:, 1:2] + wide[:, 2:3]
    label = (wide[:, 3:4] * 32.0 + wide[:, 4:5]).astype(jnp.int32)
    return half, label, wide[:, 5:6]


def prep_kernel(block_ref, member_ref, half_ref, count_ref):
    rows = block_ref.shape[0]
    meta = block_ref[:, D:]
    lane = lax.broadcasted_iota(jnp.int32, (8, META), 1)
    pick = jnp.where(lane < 3, 1.0, 0.0).astype(BF16)
    half_ref[...] = lax.dot_general(pick, meta, TRANSPOSED, preferred_element_type=F32)
    _, label, _ = split_meta(meta)
    ids = lax.broadcasted_iota(jnp.int32, (rows, CLUSTERS), 1)
    member = jnp.where(label == ids, 1.0, 0.0)
    count_ref[...] = jnp.sum(member, axis=0, keepdims=True)
    member_ref[...] = member.astype(BF16)


def prep(block):
    rows = block.shape[0]
    outs = (
        shape((rows, CLUSTERS), BF16),
        shape((8, rows), F32),
        shape((1, CLUSTERS), F32),
    )
    return call(prep_kernel, outs, (rows * CLUSTERS * 4, rows * 4096), block)


def main_kernel(blocks, rows_ref, *refs):
    block_refs, refs = refs[:blocks], refs[blocks:]
    member_refs, refs = refs[:blocks], refs[blocks:]
    half_refs, refs = refs[:blocks], refs[blocks:]
    count_refs, refs = refs[:blocks], refs[blocks:]
    out_ref, total_ref = refs
    half, label, offset = split_meta(rows_ref[:, D:])
    right = jnp.concatenate([ref[:, :D] for ref in block_refs], axis=0)
    member = jnp.concatenate([ref[...] for ref in member_refs], axis=0)
    half_row = jnp.concatenate([ref[0:1, :] for ref in half_refs], axis=1)
    count = functools.reduce(jnp.add, [ref[...] for ref in count_refs])
    gram = lax.dot_general(rows_ref[:, :D], right, TRANSPOSED, preferred_element_type=F32)
    kernel = jnp.exp2(gram * SCALE - half - half_row) - offset
    sums = jnp.dot(kernel.astype(BF16), member, preferred_element_type=F32)
    ids = lax.broadcasted_iota(jnp.int32, sums.shape, 1)
    own = jnp.where(label == ids, sums + offset * count, 0.0)
    total_ref[...] = jnp.sum(own, axis=0, keepdims=True)
    out_ref[...] = sums.astype(out_ref.dtype)


def main(rows, dtype, blocks, members, halves, counts):
    outs = (shape((rows.shape[0], CLUSTERS), dtype), shape((1, CLUSTERS), F32))
    flops = 4 * rows.shape[0] * 1280 * 1024
    size = sum(a.size * 2 for a in (rows, *blocks, *members))
    return call(
        functools.partial(main_kernel, len(blocks)),
        outs, (flops, size), rows, *blocks, *members, *halves, *counts,
    )


def sums_kernel(totals, *refs):
    out_ref = refs[-1]
    total = functools.reduce(jnp.add, [ref[...] for ref in refs[:totals]])
    count = functools.reduce(jnp.add, [ref[...] for ref in refs[totals:-1]])
    out_ref[0:1, :] = total
    out_ref[1:2, :] = count * (1.0 / 16.0)


def final_kernel(own_ref, packed_ref, sums_ref, *refs):
    out_ref = refs[-1]
    similar = own_ref[...]
    for ref in refs[:-1]:
        similar = similar + ref[...].astype(F32)
    _, _, offset = split_meta(packed_ref[:, D:])
    totals = sums_ref[0:1, :]
    counts = sums_ref[1:2, :]
    sizes = jnp.maximum(counts, 1.0)
    inverse = 1.0 / sizes
    similar = similar + offset * counts
    out_ref[...] = 1.0 - 2.0 * (similar * inverse) + totals * inverse * inverse


def merge_kernel(own_ref, first_ref, second_ref, third_ref, own_out, *outs):
    sums = own_ref[...]
    for ref in (first_ref, second_ref, third_ref):
        sums = sums + ref[...].astype(F32)
    own_out[...] = sums[:ROWS]
    for place, ref in enumerate(outs):
        ref[...] = sums[(place + 1) * ROWS : (place + 2) * ROWS].astype(BF16)


def gate_kernel(*refs):
    del refs


def gate(value, *after):
    return pl.pallas_call(
        gate_kernel,
        out_shape=shape(value.shape, value.dtype),
        in_specs=[pl.BlockSpec(memory_space=pl.ANY)] * (1 + len(after)),
        out_specs=pl.BlockSpec(memory_space=pl.ANY),
        input_output_aliases={0: 0},
    )(value, *after)


def local(clips, labels):
    def shift(value, axis, step, flip=False):
        names = axis if isinstance(axis, tuple) else (axis,)
        size = 1
        for name in names:
            size *= SIZES[AXES.index(name)]
        pairs = [(i, i ^ step if flip else (i + step) % size) for i in range(size)]
        return lax.ppermute(value, axis, pairs)

    def plane_shift(value, stage, step):
        pairs = []
        for y in range(4):
            for core in range(2):
                for x in range(4):
                    if (core == 0) == (stage == 1):
                        to_y, to_x = y, (x + step) % 4
                    else:
                        to_y, to_x = (y + step) % 4, x
                    pairs.append(((y * 2 + core) * 4 + x, (to_y * 2 + core) * 4 + to_x))
        return lax.ppermute(value, PLANE, pairs)

    def far_shift(value):
        pairs = []
        for core in range(2):
            for z in range(8):
                to_z = (z + (2 if core == 0 else -2)) % 8
                pairs.append((z // 2 * 4 + core * 2 + z % 2, to_z // 2 * 4 + core * 2 + to_z % 2))
        return lax.ppermute(value, ("z_hi", "core", "z_lo"), pairs)

    own = call(
        pack_kernel, shape((ROWS, WIDE), BF16), (10**6, ROWS * WIDE * 4),
        clips, labels.reshape(1, ROWS),
    )
    steps = (1, -1, 2)
    near = [plane_shift(own, 1, step) for step in steps]
    up = [own, shift(own, Z, 1), shift(own, Z, 2)]
    down = [own, shift(own, Z, -1), shift(own, Z, -2)]
    up.append(shift(up[2], Z, 1))
    down.append(shift(down[2], Z, -1))
    up.append(far_shift(jnp.where(lax.axis_index("core") == 0, up[2], down[2])))
    four = jnp.concatenate([own, *near], axis=0)
    rows = [plane_shift(four, 2, step) for step in steps]

    blocks = [
        jnp.concatenate([own, up[1], down[1], up[2]], axis=0),
        jnp.concatenate([down[2], up[3], down[3], up[4]], axis=0),
    ]
    blocks[1] = gate(blocks[1], *rows)
    blocks += [shift(block, "core", 1) for block in blocks]
    members, halves, counts = zip(*[prep(block) for block in blocks])

    received, totals = [], []
    for step, block in zip(steps, rows):
        sums, total = main(block, BF16, blocks, members, halves, counts)
        received.append(plane_shift(sums, 2, -step))
        totals.append(total)
    similar, total = main(four, F32, blocks, members, halves, counts)
    totals.append(total)

    sums = call(
        functools.partial(sums_kernel, 4), shape((2, CLUSTERS), F32), (10**5, 10**5),
        *totals, *counts,
    )
    sums = gate(sums, received[0], received[1])
    for step in (1, 2, 4):
        sums = sums + shift(sums, Z, step, flip=True)
    sums = sums + shift(sums, "core", 1)
    for axis in ("x", "y"):
        parts = [shift(sums, axis, step) for step in (1, 2, 3)]
        sums = sums + parts[0] + parts[1] + parts[2]

    similar, *parts = call(
        merge_kernel,
        (shape((ROWS, CLUSTERS), F32),) + (shape((ROWS, CLUSTERS), BF16),) * 3,
        (10**6, 4 * 10**6), similar, *received,
    )
    parts = [plane_shift(part, 1, -step) for step, part in zip(steps, parts)]
    return call(
        final_kernel, shape((ROWS, CLUSTERS), F32), (10**6, 2 * 10**6),
        similar, own, sums, *parts,
    )


def solution(mesh):
    fine = Mesh(mesh.devices.reshape(SIZES), AXES)
    return jax.shard_map(
        local, mesh=fine, in_specs=(P(AXES, None), P(AXES)), out_specs=P(AXES, None), check_vma=False
    )
```

profile of v0, /device:TPU:6, one launch (start us, length us, event | category | flops | bytes accessed | tf_op | source)
XLA Modules:
  0.0 118.6 jit_solution(6406413846025021905)
XLA Ops:
  0.0 0.9 copy-done.14
  1.9 3.3 %collective-permute-start.5 = (bf16[80,1152]{1,0:T(8,128)(2,1)S(1)}, bf16[80,1152]{1,0:T(8,128)(2,1)S(1)}, u32[]{:S(2)}, u32[]{:S(2)}) collective-permute-start(bf16[80,1152]{1,0:T(8,128)(2,1)S(1)} %shard_map.28.packed_ref), channel_id=1, source_target_pairs={{0,64},{4,68},{64,128},{68,132},{128,192},{132,196},{192,0},{196,4... | collective-permute-start | bytes 552968 | tf_op jit(solution)/shard_map/ppermute | solution.py:177
  5.2 2.7 %collective-permute-start.4 = (bf16[80,1152]{1,0:T(8,128)(2,1)S(1)}, bf16[80,1152]{1,0:T(8,128)(2,1)S(1)}, u32[]{:S(2)}, u32[]{:S(2)}) collective-permute-start(bf16[80,1152]{1,0:T(8,128)(2,1)S(1)} %shard_map.28.packed_ref), channel_id=1, source_target_pairs={{0,196},{4,0},{64,4},{68,64},{128,68},{132,128},{192,132},{196,192... | collective-permute-start | bytes 552968 | tf_op jit(solution)/shard_map/ppermute | solution.py:177
  7.9 1.4 %collective-permute-start.2 = (bf16[80,1152]{1,0:T(8,128)(2,1)S(1)}, bf16[80,1152]{1,0:T(8,128)(2,1)S(1)}, u32[]{:S(2)}, u32[]{:S(2)}) collective-permute-start(bf16[80,1152]{1,0:T(8,128)(2,1)S(1)} %shard_map.28.packed_ref), channel_id=1, source_target_pairs={{0,2},{1,3},{2,0},{3,1},{8,40},{9,41},{10,42},{11,43},{16,18},{17,... | collective-permute-start | bytes 552968 | tf_op jit(solution)/shard_map/ppermute | solution.py:189
  9.3 7.8 %collective-permute-done.5 = bf16[80,1152]{1,0:T(8,128)(2,1)S(1)} collective-permute-done((bf16[80,1152]{1,0:T(8,128)(2,1)S(1)}, bf16[80,1152]{1,0:T(8,128)(2,1)S(1)}, u32[]{:S(2)}, u32[]{:S(2)}) %collective-permute-start.5) | collective-permute-done | bytes 184352 | tf_op jit(solution)/shard_map/ppermute | solution.py:177
  17.6 3.3 %collective-permute-start.6 = (bf16[80,1152]{1,0:T(8,128)(2,1)S(1)}, bf16[80,1152]{1,0:T(8,128)(2,1)S(1)}, u32[]{:S(2)}, u32[]{:S(2)}) collective-permute-start(bf16[80,1152]{1,0:T(8,128)(2,1)S(1)} %shard_map.28.packed_ref), channel_id=1, source_target_pairs={{0,192},{4,196},{64,0},{68,4},{128,64},{132,68},{192,128},{196,132... | collective-permute-start | bytes 552968 | tf_op jit(solution)/shard_map/ppermute | solution.py:177
  21.0 2.3 %collective-permute-done = bf16[80,1152]{1,0:T(8,128)(2,1)S(1)} collective-permute-done((bf16[80,1152]{1,0:T(8,128)(2,1)S(1)}, bf16[80,1152]{1,0:T(8,128)(2,1)S(1)}, u32[]{:S(2)}, u32[]{:S(2)}) %collective-permute-start) | collective-permute-done | bytes 184352 | tf_op jit(solution)/shard_map/ppermute | solution.py:189
  23.4 3.3 %collective-permute-start.12 = (bf16[320,1152]{1,0:T(8,128)(2,1)S(1)}, bf16[320,1152]{1,0:T(8,128)(2,1)S(1)}, u32[]{:S(2)}, u32[]{:S(2)}) collective-permute-start(bf16[320,1152]{1,0:T(8,128)(2,1)S(1)} %get-tuple-element.54.rows_ref), channel_id=1, source_target_pairs={{0,32},{1,33},{2,34},{3,35},{8,10},{9,11},{10,8},{11,9},{16,48},{1... | collective-permute-start | bytes 2211848 | tf_op jit(solution)/shard_map/ppermute | solution.py:189
  26.7 1.0 collective-permute-start.11
  27.7 1.0 collective-permute-start.10
  28.7 1.4 %collective-permute-start.8 = (bf16[80,1152]{1,0:T(8,128)(2,1)S(1)}, bf16[80,1152]{1,0:T(8,128)(2,1)S(1)}, u32[]{:S(2)}, u32[]{:S(2)}) collective-permute-start(bf16[80,1152]{1,0:T(8,128)(2,1)S(1)} %collective-permute-done.6), channel_id=1, source_target_pairs={{0,196},{4,0},{64,4},{68,64},{128,68},{132,128},{192,132},{196,192... | collective-permute-start | bytes 552968 | tf_op jit(solution)/shard_map/ppermute | solution.py:177
  30.1 1.3 %collective-permute-start.9 = (bf16[80,1152]{1,0:T(8,128)(2,1)S(1)}, bf16[80,1152]{1,0:T(8,128)(2,1)S(1)}, u32[]{:S(2)}, u32[]{:S(2)}) collective-permute-start(bf16[80,1152]{1,0:T(8,128)(2,1)S(1)} %broadcast_select_fusion), channel_id=1, source_target_pairs={{0,64},{4,68},{64,128},{68,132},{128,192},{132,196},{192,0},{196,4... | collective-permute-start | bytes 552968 | tf_op jit(solution)/shard_map/ppermute | solution.py:197
  31.4 5.6 %collective-permute-done.8 = bf16[80,1152]{1,0:T(8,128)(2,1)S(1)} collective-permute-done((bf16[80,1152]{1,0:T(8,128)(2,1)S(1)}, bf16[80,1152]{1,0:T(8,128)(2,1)S(1)}, u32[]{:S(2)}, u32[]{:S(2)}) %collective-permute-start.8) | collective-permute-done | bytes 184352 | tf_op jit(solution)/shard_map/ppermute | solution.py:177
  37.6 4.7 %collective-permute-done.9 = bf16[80,1152]{1,0:T(8,128)(2,1)S(1)} collective-permute-done((bf16[80,1152]{1,0:T(8,128)(2,1)S(1)}, bf16[80,1152]{1,0:T(8,128)(2,1)S(1)}, u32[]{:S(2)}, u32[]{:S(2)}) %collective-permute-start.9) | collective-permute-done | bytes 184352 | tf_op jit(solution)/shard_map/ppermute | solution.py:197
  42.3 2.0 %collective-permute-done.7 = bf16[80,1152]{1,0:T(8,128)(2,1)S(1)} collective-permute-done((bf16[80,1152]{1,0:T(8,128)(2,1)S(1)}, bf16[80,1152]{1,0:T(8,128)(2,1)S(1)}, u32[]{:S(2)}, u32[]{:S(2)}) %collective-permute-start.7) | collective-permute-done | bytes 184352 | tf_op jit(solution)/shard_map/ppermute | solution.py:177
  44.2 0.9 pad_maximum_fusion.2.refs_0_
  45.2 0.9 copy-done.2
  46.0 0.9 copy-done.4
  47.2 1.1 copy-done
  49.7 3.2 %shard_map.36 = (bf16[320,1024]{1,0:T(8,128)(2,1)S(1)}, f32[1,1024]{1,0:T(1,128)S(1)}) custom-call(bf16[320,1152]{1,0:T(8,128)(2,1)} %collective-permute-done.11.refs_2_.rows_ref, bf16[320,1152]{1,0:T(8,128)(2,1)S(1)} %get-tuple-element.53.block_ref.refs_0_, bf16[320,1152]{1,0:T(8,128)(2,1)S(1)} %copy-done.1, ...), custom_call_target="tpu_custom_call" | custom-call | tf_op jit(solution)/shard_map/pallas_call | solution.py:28
  53.1 2.1 %shard_map.35 = (bf16[320,1024]{1,0:T(8,128)(2,1)S(1)}, f32[1,1024]{1,0:T(1,128)S(1)}) custom-call(bf16[320,1152]{1,0:T(8,128)(2,1)S(1)} %copy-done.5, bf16[320,1152]{1,0:T(8,128)(2,1)S(1)} %get-tuple-element.53.block_ref.refs_0_, bf16[320,1152]{1,0:T(8,128)(2,1)S(1)} %copy-done.1, bf16[320,1152]{1,0:T(8,128)(2,1)S(1)} %collective-permute-done.13.block_ref.refs_2_, ...), custom_call_target="tpu_custom_call" | custom-call | tf_op jit(solution)/shard_map/pallas_call | solution.py:28
  55.1 3.2 %collective-permute-start.15 = (bf16[320,1024]{1,0:T(8,128)(2,1)S(1)}, bf16[320,1024]{1,0:T(8,128)(2,1)S(1)}, u32[]{:S(2)}, u32[]{:S(2)}) collective-permute-start(bf16[320,1024]{1,0:T(8,128)(2,1)S(1)} %get-tuple-element.42), channel_id=1, source_target_pairs={{0,48},{1,49},{2,50},{3,51},{8,11},{9,8},{10,9},{11,10},{16,0},{17... | collective-permute-start | bytes 1966088 | tf_op jit(solution)/shard_map/ppermute | solution.py:189
  58.4 2.9 %shard_map.37 = (bf16[320,1024]{1,0:T(8,128)(2,1)}, f32[1,1024]{1,0:T(1,128)S(1)}) custom-call(bf16[320,1152]{1,0:T(8,128)(2,1)S(1)} %copy-done.3, bf16[320,1152]{1,0:T(8,128)(2,1)S(1)} %get-tuple-element.53.block_ref.refs_0_, bf16[320,1152]{1,0:T(8,128)(2,1)S(1)} %copy-done.1, bf16[320,1152]{1,0:T(8,128)(2,1)S(1)} %collective-permute-done.13.block_ref.refs_2_, ...), custom_call_target="tpu_custom_call" | custom-call | tf_op jit(solution)/shard_map/pallas_call | solution.py:28
  61.8 2.0 %shard_map.34 = (f32[320,1024]{1,0:T(8,128)S(1)}, f32[1,1024]{1,0:T(1,128)S(1)}) custom-call(bf16[320,1152]{1,0:T(8,128)(2,1)S(1)} %copy-done.7, bf16[320,1152]{1,0:T(8,128)(2,1)S(1)} %get-tuple-element.53.block_ref.refs_0_, bf16[320,1152]{1,0:T(8,128)(2,1)S(1)} %copy-done.1, bf16[320,1152]{1,0:T(8,128)(2,1)S(1)} %collective-permute-done.13.block_ref.refs_2_, ...), custom_call_target="tpu_custom_call" | custom-call | tf_op jit(solution)/shard_map/pallas_call | solution.py:28
  63.9 1.1 copy-done.12
  65.6 7.9 %collective-permute-done.15.first_ref.refs_1_ = bf16[320,1024]{1,0:T(8,128)(2,1)S(1)} collective-permute-done((bf16[320,1024]{1,0:T(8,128)(2,1)S(1)}, bf16[320,1024]{1,0:T(8,128)(2,1)S(1)}, u32[]{:S(2)}, u32[]{:S(2)}) %collective-permute-start.15) | collective-permute-done | bytes 655392 | tf_op jit(solution)/shard_map/ppermute | solution.py:189
  73.5 0.8 copy-done.10
  74.4 3.9 %collective-permute-done.18 = f32[2,1024]{1,0:T(2,128)S(1)} collective-permute-done((f32[2,1024]{1,0:T(2,128)}, f32[2,1024]{1,0:T(2,128)S(1)}, u32[]{:S(2)}, u32[]{:S(2)}) %collective-permute-start.18) | collective-permute-done | bytes 8224 | tf_op jit(solution)/shard_map/ppermute | solution.py:177
  79.0 1.2 collective-permute-start.19
  80.1 3.4 %collective-permute-done.19 = f32[2,1024]{1,0:T(2,128)S(1)} collective-permute-done((f32[2,1024]{1,0:T(2,128)S(1)}, f32[2,1024]{1,0:T(2,128)S(1)}, u32[]{:S(2)}, u32[]{:S(2)}) %collective-permute-start.19) | collective-permute-done | bytes 8224 | tf_op jit(solution)/shard_map/ppermute | solution.py:177
  83.5 5.7 %collective-permute-start.20 = (f32[2,1024]{1,0:T(2,128)S(1)}, f32[2,1024]{1,0:T(2,128)S(1)}, u32[]{:S(2)}, u32[]{:S(2)}) collective-permute-start(f32[2,1024]{1,0:T(2,128)S(1)} %add.31), channel_id=1, source_target_pairs={{0,128},{4,132},{64,192},{68,196},{128,0},{132,4},{192,64},{196,68... | collective-permute-start | bytes 24584 | tf_op jit(solution)/shard_map/ppermute | solution.py:177
  89.3 1.8 %collective-permute-done.20 = f32[2,1024]{1,0:T(2,128)S(1)} collective-permute-done((f32[2,1024]{1,0:T(2,128)S(1)}, f32[2,1024]{1,0:T(2,128)S(1)}, u32[]{:S(2)}, u32[]{:S(2)}) %collective-permute-start.20) | collective-permute-done | bytes 8224 | tf_op jit(solution)/shard_map/ppermute | solution.py:177
  91.1 1.2 collective-permute-done.21
  93.0 2.5 %collective-permute-start.23 = (f32[2,1024]{1,0:T(2,128)S(1)}, f32[2,1024]{1,0:T(2,128)S(1)}, u32[]{:S(2)}, u32[]{:S(2)}) collective-permute-start(f32[2,1024]{1,0:T(2,128)S(1)} %add.33), channel_id=1, source_target_pairs={{0,2},{1,3},{2,0},{3,1},{4,6},{5,7},{6,4},{7,5},{8,10},{9,11},{10,... | collective-permute-start | bytes 24584 | tf_op jit(solution)/shard_map/ppermute | solution.py:177
  95.8 1.4 %collective-permute-done.24 = f32[2,1024]{1,0:T(2,128)S(1)} collective-permute-done((f32[2,1024]{1,0:T(2,128)S(1)}, f32[2,1024]{1,0:T(2,128)S(1)}, u32[]{:S(2)}, u32[]{:S(2)}) %collective-permute-start.24) | collective-permute-done | bytes 8224 | tf_op jit(solution)/shard_map/ppermute | solution.py:177
  97.2 1.0 collective-permute-done.23
  98.2 1.0 collective-permute-done.22
  99.2 3.8 %collective-permute-start.27 = (f32[2,1024]{1,0:T(2,128)S(1)}, f32[2,1024]{1,0:T(2,128)S(1)}, u32[]{:S(2)}, u32[]{:S(2)}) collective-permute-start(f32[2,1024]{1,0:T(2,128)S(1)} %add_add_fusion.1), channel_id=1, source_target_pairs={{0,48},{16,0},{32,16},{48,32},{1,49},{17,1},{33,17},{49,33},{2,50}... | collective-permute-start | bytes 24584 | tf_op jit(solution)/shard_map/ppermute | solution.py:177
  102.9 1.0 collective-permute-start.25
  103.9 1.1 copy-done.9
  105.0 1.1 copy-done.11
  106.1 1.4 %shard_map.38 = (f32[80,1024]{1,0:T(8,128)S(1)}, bf16[80,1024]{1,0:T(8,128)(2,1)S(1)}, bf16[80,1024]{1,0:T(8,128)(2,1)S(1)}, bf16[80,1024]{1,0:T(8,128)(2,1)S(1)}) custom-call(f32[320,1024]{1,0:T(8,128)S(1)} %copy-done.13, bf16[320,1024]{1,0:T(8,128)(2,1)S(1)} %copy-done.11, bf16[320,1024]{1,0:T(8,128)(2,1)S(1)} %copy-done.9, ...), custom_call_target="tpu_custom_call" | custom-call | tf_op jit(solution)/shard_map/pallas_call | solution.py:28
  107.5 0.9 collective-permute-start.28
  108.4 2.4 %collective-permute-start.29 = (bf16[80,1024]{1,0:T(8,128)(2,1)S(1)}, bf16[80,1024]{1,0:T(8,128)(2,1)S(1)}, u32[]{:S(2)}, u32[]{:S(2)}) collective-permute-start(bf16[80,1024]{1,0:T(8,128)(2,1)S(1)} %get-tuple-element.51), channel_id=1, source_target_pairs={{0,1},{1,2},{2,3},{3,0},{8,24},{9,25},{10,26},{11,27},{16,17},{17,... | collective-permute-start | bytes 491528 | tf_op jit(solution)/shard_map/ppermute | solution.py:189
  111.1 3.0 %collective-permute-done.28.refs_0_ = bf16[80,1024]{1,0:T(8,128)(2,1)S(1)} collective-permute-done((bf16[80,1024]{1,0:T(8,128)(2,1)S(1)}, bf16[80,1024]{1,0:T(8,128)(2,1)S(1)}, u32[]{:S(2)}, u32[]{:S(2)}) %collective-permute-start.28) | collective-permute-done | bytes 163872 | tf_op jit(solution)/shard_map/ppermute | solution.py:189
  114.1 1.3 %collective-permute-done.29.refs_1_ = bf16[80,1024]{1,0:T(8,128)(2,1)S(1)} collective-permute-done((bf16[80,1024]{1,0:T(8,128)(2,1)S(1)}, bf16[80,1024]{1,0:T(8,128)(2,1)S(1)}, u32[]{:S(2)}, u32[]{:S(2)}) %collective-permute-start.29) | collective-permute-done | bytes 163872 | tf_op jit(solution)/shard_map/ppermute | solution.py:189
  115.4 2.2 %collective-permute-done.30.refs_2_ = bf16[80,1024]{1,0:T(8,128)(2,1)S(1)} collective-permute-done((bf16[80,1024]{1,0:T(8,128)(2,1)S(1)}, bf16[80,1024]{1,0:T(8,128)(2,1)S(1)}, u32[]{:S(2)}, u32[]{:S(2)}) %collective-permute-start.30) | collective-permute-done | bytes 163872 | tf_op jit(solution)/shard_map/ppermute | solution.py:189
  117.6 0.9 shard_map.41
  (71 shorter events, 7.3 us)
Async XLA Ops:
  0.0 0.9 copy-start.14
  0.9 0.7 copy-start.16
  1.9 15.3 %collective-permute-start.5 = (bf16[80,1152]{1,0:T(8,128)(2,1)S(1)}, bf16[80,1152]{1,0:T(8,128)(2,1)S(1)}, u32[]{:S(2)}, u32[]{:S(2)}) collective-permute-start(bf16[80,1152]{1,0:T(8,128)(2,1)S(1)} %shard_map.28.packed_ref), channel_id=1, source_target_pairs={{0,64},{4,68},{64,128},{68,132},{128,192},{132,196},{192,0},{196,4... | collective-permute-start | bytes 552968 | tf_op jit(solution)/shard_map/ppermute | solution.py:177
  5.2 12.4 %collective-permute-start.4 = (bf16[80,1152]{1,0:T(8,128)(2,1)S(1)}, bf16[80,1152]{1,0:T(8,128)(2,1)S(1)}, u32[]{:S(2)}, u32[]{:S(2)}) collective-permute-start(bf16[80,1152]{1,0:T(8,128)(2,1)S(1)} %shard_map.28.packed_ref), channel_id=1, source_target_pairs={{0,196},{4,0},{64,4},{68,64},{128,68},{132,128},{192,132},{196,192... | collective-permute-start | bytes 552968 | tf_op jit(solution)/shard_map/ppermute | solution.py:177
  7.9 13.1 %collective-permute-start.3 = (bf16[80,1152]{1,0:T(8,128)(2,1)S(1)}, bf16[80,1152]{1,0:T(8,128)(2,1)S(1)}, u32[]{:S(2)}, u32[]{:S(2)}) collective-permute-start(bf16[80,1152]{1,0:T(8,128)(2,1)S(1)} %shard_map.28.packed_ref), channel_id=1, source_target_pairs={{0,4},{4,64},{64,68},{68,128},{128,132},{132,192},{192,196},{196,0... | collective-permute-start | bytes 552968 | tf_op jit(solution)/shard_map/ppermute | solution.py:177
  7.9 13.1 %collective-permute-start.2 = (bf16[80,1152]{1,0:T(8,128)(2,1)S(1)}, bf16[80,1152]{1,0:T(8,128)(2,1)S(1)}, u32[]{:S(2)}, u32[]{:S(2)}) collective-permute-start(bf16[80,1152]{1,0:T(8,128)(2,1)S(1)} %shard_map.28.packed_ref), channel_id=1, source_target_pairs={{0,2},{1,3},{2,0},{3,1},{8,40},{9,41},{10,42},{11,43},{16,18},{17,... | collective-permute-start | bytes 552968 | tf_op jit(solution)/shard_map/ppermute | solution.py:189
  9.3 11.7 %collective-permute-start.1 = (bf16[80,1152]{1,0:T(8,128)(2,1)S(1)}, bf16[80,1152]{1,0:T(8,128)(2,1)S(1)}, u32[]{:S(2)}, u32[]{:S(2)}) collective-permute-start(bf16[80,1152]{1,0:T(8,128)(2,1)S(1)} %shard_map.28.packed_ref), channel_id=1, source_target_pairs={{0,3},{1,0},{2,1},{3,2},{8,56},{9,57},{10,58},{11,59},{16,19},{17,... | collective-permute-start | bytes 552968 | tf_op jit(solution)/shard_map/ppermute | solution.py:189
  17.1 6.1 %collective-permute-start = (bf16[80,1152]{1,0:T(8,128)(2,1)S(1)}, bf16[80,1152]{1,0:T(8,128)(2,1)S(1)}, u32[]{:S(2)}, u32[]{:S(2)}) collective-permute-start(bf16[80,1152]{1,0:T(8,128)(2,1)S(1)} %shard_map.28.packed_ref), channel_id=1, source_target_pairs={{0,1},{1,2},{2,3},{3,0},{8,24},{9,25},{10,26},{11,27},{16,17},{17,... | collective-permute-start | bytes 552968 | tf_op jit(solution)/shard_map/ppermute | solution.py:189
  17.6 11.1 %collective-permute-start.6 = (bf16[80,1152]{1,0:T(8,128)(2,1)S(1)}, bf16[80,1152]{1,0:T(8,128)(2,1)S(1)}, u32[]{:S(2)}, u32[]{:S(2)}) collective-permute-start(bf16[80,1152]{1,0:T(8,128)(2,1)S(1)} %shard_map.28.packed_ref), channel_id=1, source_target_pairs={{0,192},{4,196},{64,0},{68,4},{128,64},{132,68},{192,128},{196,132... | collective-permute-start | bytes 552968 | tf_op jit(solution)/shard_map/ppermute | solution.py:177
  23.4 21.8 %copy-start.6 = (bf16[320,1152]{1,0:T(8,128)(2,1)}, bf16[320,1152]{1,0:T(8,128)(2,1)S(1)}, u32[]{:S(2)}) copy-start(bf16[320,1152]{1,0:T(8,128)(2,1)S(1)} %get-tuple-element.54.rows_ref) | copy-start | bytes 2211844
  23.4 21.8 %collective-permute-start.12 = (bf16[320,1152]{1,0:T(8,128)(2,1)S(1)}, bf16[320,1152]{1,0:T(8,128)(2,1)S(1)}, u32[]{:S(2)}, u32[]{:S(2)}) collective-permute-start(bf16[320,1152]{1,0:T(8,128)(2,1)S(1)} %get-tuple-element.54.rows_ref), channel_id=1, source_target_pairs={{0,32},{1,33},{2,34},{3,35},{8,10},{9,11},{10,8},{11,9},{16,48},{1... | collective-permute-start | bytes 2211848 | tf_op jit(solution)/shard_map/ppermute | solution.py:189
  26.7 18.5 %collective-permute-start.11 = (bf16[320,1152]{1,0:T(8,128)(2,1)S(1)}, bf16[320,1152]{1,0:T(8,128)(2,1)}, u32[]{:S(2)}, u32[]{:S(2)}) collective-permute-start(bf16[320,1152]{1,0:T(8,128)(2,1)S(1)} %get-tuple-element.54.rows_ref), channel_id=1, source_target_pairs={{0,48},{1,49},{2,50},{3,51},{8,11},{9,8},{10,9},{11,10},{16,0},{17... | collective-permute-start | bytes 2211848 | tf_op jit(solution)/shard_map/ppermute | solution.py:189
  27.7 17.5 %collective-permute-start.10 = (bf16[320,1152]{1,0:T(8,128)(2,1)S(1)}, bf16[320,1152]{1,0:T(8,128)(2,1)S(1)}, u32[]{:S(2)}, u32[]{:S(2)}) collective-permute-start(bf16[320,1152]{1,0:T(8,128)(2,1)S(1)} %get-tuple-element.54.rows_ref), channel_id=1, source_target_pairs={{0,16},{1,17},{2,18},{3,19},{8,9},{9,10},{10,11},{11,8},{16,32},{1... | collective-permute-start | bytes 2211848 | tf_op jit(solution)/shard_map/ppermute | solution.py:189
  28.7 8.3 %collective-permute-start.8 = (bf16[80,1152]{1,0:T(8,128)(2,1)S(1)}, bf16[80,1152]{1,0:T(8,128)(2,1)S(1)}, u32[]{:S(2)}, u32[]{:S(2)}) collective-permute-start(bf16[80,1152]{1,0:T(8,128)(2,1)S(1)} %collective-permute-done.6), channel_id=1, source_target_pairs={{0,196},{4,0},{64,4},{68,64},{128,68},{132,128},{192,132},{196,192... | collective-permute-start | bytes 552968 | tf_op jit(solution)/shard_map/ppermute | solution.py:177
  30.1 12.2 %collective-permute-start.9 = (bf16[80,1152]{1,0:T(8,128)(2,1)S(1)}, bf16[80,1152]{1,0:T(8,128)(2,1)S(1)}, u32[]{:S(2)}, u32[]{:S(2)}) collective-permute-start(bf16[80,1152]{1,0:T(8,128)(2,1)S(1)} %broadcast_select_fusion), channel_id=1, source_target_pairs={{0,64},{4,68},{64,128},{68,132},{128,192},{132,196},{192,0},{196,4... | collective-permute-start | bytes 552968 | tf_op jit(solution)/shard_map/ppermute | solution.py:197
  37.0 7.3 %collective-permute-start.7 = (bf16[80,1152]{1,0:T(8,128)(2,1)S(1)}, bf16[80,1152]{1,0:T(8,128)(2,1)S(1)}, u32[]{:S(2)}, u32[]{:S(2)}) collective-permute-start(bf16[80,1152]{1,0:T(8,128)(2,1)S(1)} %collective-permute-done.5), channel_id=1, source_target_pairs={{0,4},{4,64},{64,68},{68,128},{128,132},{132,192},{192,196},{196,0... | collective-permute-start | bytes 552968 | tf_op jit(solution)/shard_map/ppermute | solution.py:177
  42.3 6.4 %collective-permute-start.13 = (bf16[320,1152]{1,0:T(8,128)(2,1)S(1)}, bf16[320,1152]{1,0:T(8,128)(2,1)S(1)}, u32[]{:S(2)}, u32[]{:S(2)}) collective-permute-start(bf16[320,1152]{1,0:T(8,128)(2,1)S(1)} %get-tuple-element.53.block_ref.refs_0_), channel_id=1, source_target_pairs={{0,8},{8,0},{1,9},{9,1},{2,10},{10,2},{3,11},{11,3},{4,12},{12,4},... | collective-permute-start | bytes 2211848 | tf_op jit(solution)/shard_map/ppermute | solution.py:177
  45.2 0.9 copy-start.2
  46.0 0.9 copy-start.4
  46.9 2.7 %copy-start.1 = (bf16[320,1152]{1,0:T(8,128)(2,1)S(1)}, bf16[320,1152]{1,0:T(8,128)(2,1)}, u32[]{:S(2)}) copy-start(bf16[320,1152]{1,0:T(8,128)(2,1)} %shard_map.29.block_ref.refs_1_) | copy-start | bytes 2211844
  46.9 2.4 %collective-permute-start.14 = (bf16[320,1152]{1,0:T(8,128)(2,1)}, bf16[320,1152]{1,0:T(8,128)(2,1)S(1)}, u32[]{:S(2)}, u32[]{:S(2)}) collective-permute-start(bf16[320,1152]{1,0:T(8,128)(2,1)} %shard_map.29.block_ref.refs_1_), channel_id=1, source_target_pairs={{0,8},{8,0},{1,9},{9,1},{2,10},{10,2},{3,11},{11,3},{4,12},{12,4},... | collective-permute-start | bytes 2211848 | tf_op jit(solution)/shard_map/ppermute | solution.py:177
  47.2 1.1 copy-start
  49.7 3.4 %copy-start.5 = (bf16[320,1152]{1,0:T(8,128)(2,1)S(1)}, bf16[320,1152]{1,0:T(8,128)(2,1)}, u32[]{:S(2)}) copy-start(bf16[320,1152]{1,0:T(8,128)(2,1)} %copy-done.4) | copy-start | bytes 2211844
  52.9 5.5 %copy-start.3 = (bf16[320,1152]{1,0:T(8,128)(2,1)S(1)}, bf16[320,1152]{1,0:T(8,128)(2,1)}, u32[]{:S(2)}) copy-start(bf16[320,1152]{1,0:T(8,128)(2,1)} %copy-done.2) | copy-start | bytes 2211844
  52.9 12.7 %collective-permute-start.16 = (bf16[320,1024]{1,0:T(8,128)(2,1)S(1)}, bf16[320,1024]{1,0:T(8,128)(2,1)S(1)}, u32[]{:S(2)}, u32[]{:S(2)}) collective-permute-start(bf16[320,1024]{1,0:T(8,128)(2,1)S(1)} %get-tuple-element.43), channel_id=1, source_target_pairs={{0,16},{1,17},{2,18},{3,19},{8,9},{9,10},{10,11},{11,8},{16,32},{1... | collective-permute-start | bytes 1966088 | tf_op jit(solution)/shard_map/ppermute | solution.py:189
  55.1 6.7 %copy-start.7 = (bf16[320,1152]{1,0:T(8,128)(2,1)S(1)}, bf16[320,1152]{1,0:T(8,128)(2,1)}, u32[]{:S(2)}) copy-start(bf16[320,1152]{1,0:T(8,128)(2,1)} %copy-done.6) | copy-start | bytes 2211844
  55.1 18.4 %collective-permute-start.15 = (bf16[320,1024]{1,0:T(8,128)(2,1)S(1)}, bf16[320,1024]{1,0:T(8,128)(2,1)S(1)}, u32[]{:S(2)}, u32[]{:S(2)}) collective-permute-start(bf16[320,1024]{1,0:T(8,128)(2,1)S(1)} %get-tuple-element.42), channel_id=1, source_target_pairs={{0,48},{1,49},{2,50},{3,51},{8,11},{9,8},{10,9},{11,10},{16,0},{17... | collective-permute-start | bytes 1966088 | tf_op jit(solution)/shard_map/ppermute | solution.py:189
  61.3 42.6 %collective-permute-start.17 = (bf16[320,1024]{1,0:T(8,128)(2,1)}, bf16[320,1024]{1,0:T(8,128)(2,1)}, u32[]{:S(2)}, u32[]{:S(2)}) collective-permute-start(bf16[320,1024]{1,0:T(8,128)(2,1)} %get-tuple-element.44), channel_id=1, source_target_pairs={{0,32},{1,33},{2,34},{3,35},{8,10},{9,11},{10,8},{11,9},{16,48},{1... | collective-permute-start | bytes 1966088 | tf_op jit(solution)/shard_map/ppermute | solution.py:189
  63.8 1.1 copy-start.12
  65.0 38.9 %copy-start.13 = (f32[320,1024]{1,0:T(8,128)S(1)}, f32[320,1024]{1,0:T(8,128)}, u32[]{:S(2)}) copy-start(f32[320,1024]{1,0:T(8,128)} %copy-done.12) | copy-start | bytes 3932164
  65.0 0.6 copy-start.15
  65.6 7.9 %copy-start.8 = (bf16[320,1024]{1,0:T(8,128)(2,1)}, bf16[320,1024]{1,0:T(8,128)(2,1)S(1)}, u32[]{:S(2)}) copy-start(bf16[320,1024]{1,0:T(8,128)(2,1)S(1)} %collective-permute-done.16.second_ref.refs_2_) | copy-start | bytes 1966084
  73.5 0.8 copy-start.10
  74.4 3.9 %collective-permute-start.18 = (f32[2,1024]{1,0:T(2,128)}, f32[2,1024]{1,0:T(2,128)S(1)}, u32[]{:S(2)}, u32[]{:S(2)}) collective-permute-start(f32[2,1024]{1,0:T(2,128)} %shard_map.40), channel_id=1, source_target_pairs={{0,4},{4,0},{64,68},{68,64},{128,132},{132,128},{192,196},{196,192... | collective-permute-start | bytes 24584 | tf_op jit(solution)/shard_map/ppermute | solution.py:177
  79.0 4.5 %collective-permute-start.19 = (f32[2,1024]{1,0:T(2,128)S(1)}, f32[2,1024]{1,0:T(2,128)S(1)}, u32[]{:S(2)}, u32[]{:S(2)}) collective-permute-start(f32[2,1024]{1,0:T(2,128)S(1)} %add.30), channel_id=1, source_target_pairs={{0,64},{4,68},{64,0},{68,4},{128,192},{132,196},{192,128},{196,132... | collective-permute-start | bytes 24584 | tf_op jit(solution)/shard_map/ppermute | solution.py:177
  83.5 7.6 %collective-permute-start.20 = (f32[2,1024]{1,0:T(2,128)S(1)}, f32[2,1024]{1,0:T(2,128)S(1)}, u32[]{:S(2)}, u32[]{:S(2)}) collective-permute-start(f32[2,1024]{1,0:T(2,128)S(1)} %add.31), channel_id=1, source_target_pairs={{0,128},{4,132},{64,192},{68,196},{128,0},{132,4},{192,64},{196,68... | collective-permute-start | bytes 24584 | tf_op jit(solution)/shard_map/ppermute | solution.py:177
  91.1 1.2 collective-permute-start.21
  92.3 4.9 %collective-permute-start.24 = (f32[2,1024]{1,0:T(2,128)S(1)}, f32[2,1024]{1,0:T(2,128)S(1)}, u32[]{:S(2)}, u32[]{:S(2)}) collective-permute-start(f32[2,1024]{1,0:T(2,128)S(1)} %add.33), channel_id=1, source_target_pairs={{0,3},{1,0},{2,1},{3,2},{4,7},{5,4},{6,5},{7,6},{8,11},{9,8},{10,9... | collective-permute-start | bytes 24584 | tf_op jit(solution)/shard_map/ppermute | solution.py:177
  93.0 5.2 %collective-permute-start.23 = (f32[2,1024]{1,0:T(2,128)S(1)}, f32[2,1024]{1,0:T(2,128)S(1)}, u32[]{:S(2)}, u32[]{:S(2)}) collective-permute-start(f32[2,1024]{1,0:T(2,128)S(1)} %add.33), channel_id=1, source_target_pairs={{0,2},{1,3},{2,0},{3,1},{4,6},{5,7},{6,4},{7,5},{8,10},{9,11},{10,... | collective-permute-start | bytes 24584 | tf_op jit(solution)/shard_map/ppermute | solution.py:177
  95.5 3.7 %collective-permute-start.22 = (f32[2,1024]{1,0:T(2,128)S(1)}, f32[2,1024]{1,0:T(2,128)S(1)}, u32[]{:S(2)}, u32[]{:S(2)}) collective-permute-start(f32[2,1024]{1,0:T(2,128)S(1)} %add.33), channel_id=1, source_target_pairs={{0,1},{1,2},{2,3},{3,0},{4,5},{5,6},{6,7},{7,4},{8,9},{9,10},{10,1... | collective-permute-start | bytes 24584 | tf_op jit(solution)/shard_map/ppermute | solution.py:177
  99.2 11.6 %collective-permute-start.27 = (f32[2,1024]{1,0:T(2,128)S(1)}, f32[2,1024]{1,0:T(2,128)S(1)}, u32[]{:S(2)}, u32[]{:S(2)}) collective-permute-start(f32[2,1024]{1,0:T(2,128)S(1)} %add_add_fusion.1), channel_id=1, source_target_pairs={{0,48},{16,0},{32,16},{48,32},{1,49},{17,1},{33,17},{49,33},{2,50}... | collective-permute-start | bytes 24584 | tf_op jit(solution)/shard_map/ppermute | solution.py:177
  102.9 8.2 %collective-permute-start.26 = (f32[2,1024]{1,0:T(2,128)S(1)}, f32[2,1024]{1,0:T(2,128)S(1)}, u32[]{:S(2)}, u32[]{:S(2)}) collective-permute-start(f32[2,1024]{1,0:T(2,128)S(1)} %add_add_fusion.1), channel_id=1, source_target_pairs={{0,32},{16,48},{32,0},{48,16},{1,33},{17,49},{33,1},{49,17},{2,34}... | collective-permute-start | bytes 24584 | tf_op jit(solution)/shard_map/ppermute | solution.py:177
  102.9 8.2 %collective-permute-start.25 = (f32[2,1024]{1,0:T(2,128)S(1)}, f32[2,1024]{1,0:T(2,128)S(1)}, u32[]{:S(2)}, u32[]{:S(2)}) collective-permute-start(f32[2,1024]{1,0:T(2,128)S(1)} %add_add_fusion.1), channel_id=1, source_target_pairs={{0,16},{16,32},{32,48},{48,0},{1,17},{17,33},{33,49},{49,1},{2,18}... | collective-permute-start | bytes 24584 | tf_op jit(solution)/shard_map/ppermute | solution.py:177
  103.9 1.1 copy-start.9
  105.0 1.1 copy-start.11
  107.5 6.6 %collective-permute-start.28 = (bf16[80,1024]{1,0:T(8,128)(2,1)S(1)}, bf16[80,1024]{1,0:T(8,128)(2,1)S(1)}, u32[]{:S(2)}, u32[]{:S(2)}) collective-permute-start(bf16[80,1024]{1,0:T(8,128)(2,1)S(1)} %get-tuple-element.50), channel_id=1, source_target_pairs={{0,3},{1,0},{2,1},{3,2},{8,56},{9,57},{10,58},{11,59},{16,19},{17,... | collective-permute-start | bytes 491528 | tf_op jit(solution)/shard_map/ppermute | solution.py:189
  108.4 7.0 %collective-permute-start.29 = (bf16[80,1024]{1,0:T(8,128)(2,1)S(1)}, bf16[80,1024]{1,0:T(8,128)(2,1)S(1)}, u32[]{:S(2)}, u32[]{:S(2)}) collective-permute-start(bf16[80,1024]{1,0:T(8,128)(2,1)S(1)} %get-tuple-element.51), channel_id=1, source_target_pairs={{0,1},{1,2},{2,3},{3,0},{8,24},{9,25},{10,26},{11,27},{16,17},{17,... | collective-permute-start | bytes 491528 | tf_op jit(solution)/shard_map/ppermute | solution.py:189
  110.8 6.8 %collective-permute-start.30 = (bf16[80,1024]{1,0:T(8,128)(2,1)S(1)}, bf16[80,1024]{1,0:T(8,128)(2,1)S(1)}, u32[]{:S(2)}, u32[]{:S(2)}) collective-permute-start(bf16[80,1024]{1,0:T(8,128)(2,1)S(1)} %get-tuple-element.52), channel_id=1, source_target_pairs={{0,2},{1,3},{2,0},{3,1},{8,40},{9,41},{10,42},{11,43},{16,18},{17,... | collective-permute-start | bytes 491528 | tf_op jit(solution)/shard_map/ppermute | solution.py:189
where the time goes:
time: 121 us; the launch traced here: 119 us
  waiting for transfers between devices  50.8 us (42%)
  starting transfers between devices  42.6 us (35%)
  Pallas kernels  14.1 us (12%)
  local copies, waits for them, and re-layouts  9.15 us (8%)
  other arithmetic  1.8 us (1%)
    ppermute x18, waiting for transfers between devices, shift(): return lax.ppermute(value, axis, pairs)  29.4 us
    ppermute x18, starting transfers between devices, shift(): return lax.ppermute(value, axis, pairs)  26.6 us
    ppermute x12, waiting for transfers between devices, plane_shift(): return lax.ppermute(value, PLANE, pairs)  16.7 us
    ppermute x12, starting transfers between devices, plane_shift(): return lax.ppermute(value, PLANE, pairs)  14.7 us
    pallas_call x12, Pallas kernels, call(): pl.pallas_call(body, out_shape=outs, compiler_params=pltpu.CompilerParams...  14.1 us
    unnamed x34, local copies, waits for them, and re-layouts  9.15 us
    ppermute x1, waiting for transfers between devices, far_shift(): return lax.ppermute(value, ('z_hi', 'core', 'z_lo'), pairs)  4.67 us
  transfers between devices with their start and end apart: 31, of which 17 were waited for; matrix products, arithmetic and copies ran while one was open for 2% of the time, Pallas kernels for 8%

commit v1 on v0

v1 whole, which is shorter than its diff:
```python
import functools

import jax
import jax.numpy as jnp
from jax import lax
from jax.experimental import pallas as pl
from jax.experimental.pallas import tpu as pltpu
from jax.sharding import Mesh, PartitionSpec as P

D = 1024
CLUSTERS = 1024
META = 128
WIDE = D + META
ROWS = 80
LOG2E = 1.4426950408889634
SCALE = LOG2E / D
F32 = jnp.float32
SMALL = 8 * 2**20
LARGE = 24 * 2**20
LONG = 3 * 10**9
BF16 = jnp.bfloat16
TRANSPOSED = (((1,), (1,)), ((), ()))
AXES = ("z_hi", "y", "core", "z_lo", "x")
SIZES = (4, 4, 2, 2, 4)
Z = ("z_hi", "z_lo")
PLANE = ("y", "core", "x")


def call(body, outs, cost, *args):
    flops, size = cost
    return pl.pallas_call(
        body,
        out_shape=outs,
        compiler_params=pltpu.CompilerParams(vmem_limit_bytes=LARGE),
        cost_estimate=pl.CostEstimate(flops=flops, bytes_accessed=size, transcendentals=0),
    )(*args)


def shape(dims, dtype):
    return jax.ShapeDtypeStruct(dims, dtype)


def pack_kernel(clips_hbm, labels_hbm, out_ref, clips_ref, labels_ref, clips_sem, labels_sem):
    clips_copy = pltpu.make_async_copy(clips_hbm, clips_ref, clips_sem)
    labels_copy = pltpu.make_async_copy(labels_hbm, labels_ref, labels_sem)
    clips_copy.start()
    labels_copy.start()
    labels_copy.wait()
    clips_copy.wait()
    x = clips_ref[...]
    wide = x.astype(F32)
    half = jnp.sum(wide * wide, axis=1, keepdims=True) * (0.5 * SCALE)
    row = lax.broadcasted_iota(jnp.int32, (ROWS, ROWS), 0)
    col = lax.broadcasted_iota(jnp.int32, (ROWS, ROWS), 1)
    same = row == col
    label = jnp.sum(jnp.where(same, labels_ref[...].astype(F32), 0.0), axis=1, keepdims=True)
    half_row = jnp.sum(jnp.where(same, half, 0.0), axis=0, keepdims=True)
    gram = lax.dot_general(x, x, TRANSPOSED, preferred_element_type=F32)
    near = jnp.exp2(gram * SCALE - half - half_row)
    offset = jnp.sum(jnp.where(same, 0.0, near), axis=1, keepdims=True) * (1.0 / (ROWS - 1))
    first = half.astype(BF16).astype(F32)
    second = (half - first).astype(BF16).astype(F32)
    third = half - first - second
    upper = jnp.floor(label * (1.0 / 32.0))
    lower = label - 32.0 * upper
    lane = lax.broadcasted_iota(jnp.int32, (ROWS, META), 1)
    meta = jnp.zeros((ROWS, META), F32)
    for place, value in enumerate((first, second, third, upper, lower, offset)):
        meta = jnp.where(lane == place, value, meta)
    out_ref[:, :D] = x
    out_ref[:, D:] = meta.astype(BF16)


def split_meta(meta):
    wide = meta.astype(F32)
    half = wide[:, 0:1] + wide[:, 1:2] + wide[:, 2:3]
    label = (wide[:, 3:4] * 32.0 + wide[:, 4:5]).astype(jnp.int32)
    return half, label, wide[:, 5:6]


def prep_kernel(block_ref, member_ref, row_ref, count_ref):
    rows = block_ref.shape[0]
    meta = block_ref[:, D:]
    line = lax.broadcasted_iota(jnp.int32, (8, META), 0)
    lane = lax.broadcasted_iota(jnp.int32, (8, META), 1)
    pick = jnp.where((line == 0) & (lane < 3), 1.0, 0.0)
    pick = jnp.where((line == 1) & (lane == 3), 32.0, pick)
    pick = jnp.where((line == 1) & (lane == 4), 1.0, pick).astype(BF16)
    row_ref[...] = lax.dot_general(pick, meta, TRANSPOSED, preferred_element_type=F32)
    _, label, _ = split_meta(meta)
    ids = lax.broadcasted_iota(jnp.int32, (rows, CLUSTERS), 1)
    member = jnp.where(label == ids, 1.0, 0.0)
    count_ref[...] = jnp.sum(member, axis=0, keepdims=True)
    member_ref[...] = member.astype(BF16)


def prep(block):
    rows = block.shape[0]
    outs = (
        shape((rows, CLUSTERS), BF16),
        shape((8, rows), F32),
        shape((1, CLUSTERS), F32),
    )
    return call(prep_kernel, outs, (0, 0), block)


def kernel_kernel(parts, blocks, *refs):
    part_refs, refs = refs[:parts], refs[parts:]
    block_refs, refs = refs[:blocks], refs[blocks:]
    row_refs, refs = refs[:blocks], refs[blocks:]
    count_refs, refs = refs[:blocks], refs[blocks:]
    out_refs, sums_ref = refs[:parts], refs[parts]
    right = jnp.concatenate([ref[:, :D] for ref in block_refs], axis=0)
    half_row = jnp.concatenate([ref[0:1, :] for ref in row_refs], axis=1)
    label_row = jnp.concatenate([ref[1:2, :] for ref in row_refs], axis=1).astype(jnp.int32)
    total = None
    for part, out in zip(part_refs, out_refs):
        half, label, offset = split_meta(part[:, D:])
        gram = lax.dot_general(part[:, :D], right, TRANSPOSED, preferred_element_type=F32)
        kernel = jnp.exp2(gram * SCALE - half - half_row)
        own = jnp.sum(jnp.where(label == label_row, kernel, 0.0), axis=1, keepdims=True)
        out[...] = (kernel - offset).astype(BF16)
        ids = lax.broadcasted_iota(jnp.int32, (part.shape[0], CLUSTERS), 1)
        term = jnp.sum(jnp.where(label == ids, own, 0.0), axis=0, keepdims=True)
        total = term if total is None else total + term
    sums_ref[0:1, :] = total
    count = functools.reduce(jnp.add, [ref[...] for ref in count_refs])
    sums_ref[1:2, :] = count * (1.0 / 16.0)


def kernels(parts, blocks, rows, counts):
    width = sum(block.shape[0] for block in blocks)
    outs = tuple(shape((part.shape[0], width), BF16) for part in parts)
    return call(
        functools.partial(kernel_kernel, len(parts), len(blocks)),
        outs + (shape((2, CLUSTERS), F32),), (0, 0), *parts, *blocks, *rows, *counts,
    )


def main_kernel(kernel_ref, *refs):
    out_ref = refs[-1]
    member = jnp.concatenate([ref[...] for ref in refs[:-1]], axis=0)
    sums = jnp.dot(kernel_ref[...], member, preferred_element_type=F32)
    out_ref[...] = sums.astype(out_ref.dtype)


def main(kernel, dtype, members):
    return call(main_kernel, shape((kernel.shape[0], CLUSTERS), dtype), (0, 0), kernel, *members)


def merge_kernel(own_ref, first_ref, second_ref, third_ref, sums_ref, own_out, *outs):
    sums = own_ref[...]
    for ref in (first_ref, second_ref, third_ref):
        sums = sums + ref[...].astype(F32)
    own_out[...] = sums[:ROWS]
    rest = sums_ref[...]
    pieces = []
    for _ in range(3):
        pieces.append(rest.astype(BF16).astype(F32))
        rest = rest - pieces[-1]
    extra = jnp.concatenate(pieces + [jnp.zeros((10, CLUSTERS), F32)], axis=0).astype(BF16)
    for place, ref in enumerate(outs):
        ref[:ROWS, :] = sums[(place + 1) * ROWS : (place + 2) * ROWS].astype(BF16)
        ref[ROWS:, :] = extra


def final_kernel(own_ref, packed_ref, sums_ref, *refs):
    out_ref = refs[-1]
    similar = own_ref[...]
    sums = sums_ref[...]
    for ref in refs[:-1]:
        similar = similar + ref[:ROWS, :].astype(F32)
        extra = ref[ROWS:, :].astype(F32)
        sums = sums + (extra[0:2] + extra[2:4] + extra[4:6])
    _, _, offset = split_meta(packed_ref[:, D:])
    totals = sums[0:1, :]
    counts = sums[1:2, :]
    sizes = jnp.maximum(counts, 1.0)
    inverse = 1.0 / sizes
    similar = similar + offset * counts
    out_ref[...] = 1.0 - 2.0 * (similar * inverse) + totals * inverse * inverse


def plus_kernel(count, *refs):
    refs[-1][...] = functools.reduce(jnp.add, [ref[...] for ref in refs[:count]])


def plus(values, after=(), flops=0):
    return call(
        functools.partial(plus_kernel, len(values)),
        shape(values[0].shape, values[0].dtype), (flops, 0), *values, *after,
    )


def relay_kernel(*refs):
    del refs


def relay(values, after=(), flops=0):
    return pl.pallas_call(
        relay_kernel,
        out_shape=[shape(value.shape, value.dtype) for value in values],
        input_output_aliases={place: place for place in range(len(values))},
        compiler_params=pltpu.CompilerParams(vmem_limit_bytes=SMALL),
        cost_estimate=pl.CostEstimate(flops=flops, bytes_accessed=0, transcendentals=0),
    )(*values, *after)


def join_kernel(count, *refs):
    refs[-1][...] = jnp.concatenate([ref[...] for ref in refs[:count]], axis=0)


def join(values, after=(), flops=0):
    rows = sum(value.shape[0] for value in values)
    return call(
        functools.partial(join_kernel, len(values)),
        shape((rows, values[0].shape[1]), values[0].dtype), (flops, 0), *values, *after,
    )


def local(clips, labels):
    def shift(value, axis, step, flip=False):
        names = axis if isinstance(axis, tuple) else (axis,)
        size = 1
        for name in names:
            size *= SIZES[AXES.index(name)]
        pairs = [(i, i ^ step if flip else (i + step) % size) for i in range(size)]
        return lax.ppermute(value, axis, pairs)

    def plane_shift(value, stage, step):
        pairs = []
        for y in range(4):
            for core in range(2):
                for x in range(4):
                    if (core == 0) == (stage == 1):
                        to_y, to_x = y, (x + step) % 4
                    else:
                        to_y, to_x = (y + step) % 4, x
                    pairs.append(((y * 2 + core) * 4 + x, (to_y * 2 + core) * 4 + to_x))
        return lax.ppermute(value, PLANE, pairs)

    own = pl.pallas_call(
        pack_kernel,
        out_shape=shape((ROWS, WIDE), BF16),
        in_specs=[pl.BlockSpec(memory_space=pl.ANY)] * 2,
        out_specs=pl.BlockSpec(memory_space=pltpu.VMEM),
        scratch_shapes=[
            pltpu.VMEM((ROWS, D), BF16),
            pltpu.VMEM((1, ROWS), jnp.int32),
            pltpu.SemaphoreType.DMA,
            pltpu.SemaphoreType.DMA,
        ],
        compiler_params=pltpu.CompilerParams(vmem_limit_bytes=SMALL),
    )(clips, labels.reshape(1, ROWS))
    steps = (1, -1, 2)
    near = [plane_shift(own, 1, step) for step in steps]
    up = [own, shift(own, Z, 1)]
    down = [own, shift(own, Z, -1)]
    four = join([own, *near], after=[up[1], down[1]], flops=10**9)
    rows = [plane_shift(four, 2, step) for step in steps]
    up.append(shift(up[1], Z, 1))
    down.append(shift(down[1], Z, -1))
    up.append(shift(up[2], Z, 1))
    down.append(shift(down[2], Z, -1))
    up.append(shift(up[3], Z, 1))

    blocks = [join([own, *up[1:4], *down[1:4]])]
    blocks += [shift(block, "core", 1) for block in blocks]
    early = [prep(block) for block in blocks]
    blocks.append(join([up[4]], after=[member for member, _, _ in early]))
    blocks.append(shift(blocks[-1], "core", 1))
    members, lines, counts = zip(*early, *[prep(block) for block in blocks[2:]])

    for _ in range(4):
        rows = relay(rows, flops=3 * 10**9)
    *kernel, sums = kernels([*rows, four], blocks, lines, counts)
    terms = [main(part, BF16, members) for part in kernel[:3]]
    received = [plane_shift(term, 2, -step) for step, term in zip(steps, terms)]
    sums = plus([sums, shift(sums, Z, 1, flip=True)], after=terms[:2], flops=LONG)
    others = [shift(sums, Z, step) for step in (2, -2, 4)]
    sums = plus([sums, *others], after=terms[2:], flops=LONG)
    sums = plus([sums, shift(sums, "core", 1)], after=received[:1], flops=LONG)
    others = [plane_shift(sums, 2, step) for step in steps]
    sums = plus([sums, *others], after=received[1:2], flops=LONG)
    similar = main(kernel[3], F32, members)
    similar, *parts = call(
        merge_kernel,
        (shape((ROWS, CLUSTERS), F32),) + (shape((ROWS + 16, CLUSTERS), BF16),) * 3,
        (0, 0), similar, *received, sums,
    )
    parts = [plane_shift(part, 1, -step) for step, part in zip(steps, parts)]
    return call(
        final_kernel, shape((ROWS, CLUSTERS), F32), (0, 0), similar, own, sums, *parts
    )


def solution(mesh):
    fine = Mesh(mesh.devices.reshape(SIZES), AXES)
    return jax.shard_map(
        local, mesh=fine, in_specs=(P(AXES, None), P(AXES)), out_specs=P(AXES, None), check_vma=False
    )
```

time: 121 us -> 86.6 us (0.72); the launches traced: 119 us -> 86.5 us
  waiting for transfers between devices: 50.8 us -> 33.8 us
  local copies, waits for them, and re-layouts: 9.15 us -> 1.57 us
  starting transfers between devices: 42.6 us -> 39.1 us
  Pallas kernels: 14.1 us -> 11.9 us
  other arithmetic: 1.8 us -> 0 us
    ppermute x18 -> x14, waiting for transfers between devices: 29.4 us -> 16.4 us  [shift(): return lax.ppermute(value, axis, pairs)]
    ppermute x18 -> x14, starting transfers between devices: 26.6 us -> 17.2 us  [shift(): return lax.ppermute(value, axis, pairs)]
    unnamed x34 -> x4, local copies, waits for them, and re-layouts: 9.15 us -> 1.57 us
    ppermute x12 -> x15, starting transfers between devices: 14.7 us -> 21.8 us  [plane_shift(): return lax.ppermute(value, PLANE, pairs)]
    ppermute x1 -> x0, waiting for transfers between devices: 4.67 us -> none  [far_shift(): return lax.ppermute(value, ('z_hi', 'core', 'z_lo'), pairs)]
    pallas_call x12 -> x18, Pallas kernels: 14.1 us -> 11.4 us  [call(): pl.pallas_call(body, out_shape=outs, compiler_params=pltpu.CompilerParams...]
    ppermute x1 -> x0, starting transfers between devices: 1.27 us -> none  [far_shift(): return lax.ppermute(value, ('z_hi', 'core', 'z_lo'), pairs)]
    ppermute x12 -> x15, waiting for transfers between devices: 16.7 us -> 17.4 us  [plane_shift(): return lax.ppermute(value, PLANE, pairs)]
  transfers between devices with their start and end apart: 31 -> 29, of which waited for: 17 -> 14; matrix products, arithmetic and copies ran while one was open for 2% -> 0% of each run, Pallas kernels for 8% -> 5%
where the time goes in v1:
time: 86.6 us; the launch traced here: 86.5 us
  starting transfers between devices  39.1 us (45%)
  waiting for transfers between devices  33.8 us (39%)
  Pallas kernels  11.9 us (14%)
  local copies, waits for them, and re-layouts  1.57 us (2%)
    ppermute x15, starting transfers between devices, plane_shift(): return lax.ppermute(value, PLANE, pairs)  21.8 us
    ppermute x15, waiting for transfers between devices, plane_shift(): return lax.ppermute(value, PLANE, pairs)  17.4 us
    ppermute x14, starting transfers between devices, shift(): return lax.ppermute(value, axis, pairs)  17.2 us
    ppermute x14, waiting for transfers between devices, shift(): return lax.ppermute(value, axis, pairs)  16.4 us
    pallas_call x18, Pallas kernels, call(): pl.pallas_call(body, out_shape=outs, compiler_params=pltpu.CompilerParams...  11.4 us
  transfers between devices with their start and end apart: 29, of which 14 were waited for; matrix products, arithmetic and copies ran while one was open for 0% of the time, Pallas kernels for 5%

profile of v1, /device:TPU:6, one launch (start us, length us, event | category | flops | bytes accessed | tf_op | source)
XLA Modules:
  0.0 86.5 jit_solution(185006290408641589)
XLA Ops:
  0.0 0.9 %copy-done = bf16[80,1024]{1,0:T(8,128)(2,1)S(1)} copy-done((bf16[80,1024]{1,0:T(8,128)(2,1)S(1)}, bf16[80,1024]{1,0:T(8,128)(2,1)}, u32[]{:S(2)}) %copy-start) | copy-done | bytes 163864
  0.9 0.7 copy-done.1
  1.6 0.5 shard_map.28.refs_0_.packed_ref
  2.1 5.9 %collective-permute-start.4 = (bf16[80,1152]{1,0:T(8,128)(2,1)S(1)}, bf16[80,1152]{1,0:T(8,128)(2,1)S(1)}, u32[]{:S(2)}, u32[]{:S(2)}) collective-permute-start(bf16[80,1152]{1,0:T(8,128)(2,1)S(1)} %shard_map.28.refs_0_.packed_ref), channel_id=1, source_target_pairs={{0,196},{4,0},{64,4},{68,64},{128,68},{132,128},{192,132},{196,192... | collective-permute-start | bytes 552968 | tf_op jit(solution)/shard_map/ppermute | solution.py:228
  8.0 1.4 %collective-permute-start.2 = (bf16[80,1152]{1,0:T(8,128)(2,1)S(1)}, bf16[80,1152]{1,0:T(8,128)(2,1)S(1)}, u32[]{:S(2)}, u32[]{:S(2)}) collective-permute-start(bf16[80,1152]{1,0:T(8,128)(2,1)S(1)} %shard_map.28.refs_0_.packed_ref), channel_id=1, source_target_pairs={{0,2},{1,3},{2,0},{3,1},{8,40},{9,41},{10,42},{11,43},{16,18},{17,... | collective-permute-start | bytes 552968 | tf_op jit(solution)/shard_map/ppermute | solution.py:240
  9.4 3.2 %collective-permute-start = (bf16[80,1152]{1,0:T(8,128)(2,1)S(1)}, bf16[80,1152]{1,0:T(8,128)(2,1)S(1)}, u32[]{:S(2)}, u32[]{:S(2)}) collective-permute-start(bf16[80,1152]{1,0:T(8,128)(2,1)S(1)} %shard_map.28.refs_0_.packed_ref), channel_id=1, source_target_pairs={{0,1},{1,2},{2,3},{3,0},{8,24},{9,25},{10,26},{11,27},{16,17},{17,... | collective-permute-start | bytes 552968 | tf_op jit(solution)/shard_map/ppermute | solution.py:240
  12.6 3.2 %collective-permute-start.10 = (bf16[80,1152]{1,0:T(8,128)(2,1)S(1)}, bf16[80,1152]{1,0:T(8,128)(2,1)S(1)}, u32[]{:S(2)}, u32[]{:S(2)}) collective-permute-start(bf16[80,1152]{1,0:T(8,128)(2,1)S(1)} %collective-permute-done.4.refs_5_.refs_4_), channel_id=1, source_target_pairs={{0,196},{4,0},{64,4},{68,64},{128,68},{132,128},{192,132},{196,192... | collective-permute-start | bytes 552968 | tf_op jit(solution)/shard_map/ppermute | solution.py:228
  15.9 1.1 %collective-permute-done.1.refs_2_ = bf16[80,1152]{1,0:T(8,128)(2,1)S(1)} collective-permute-done((bf16[80,1152]{1,0:T(8,128)(2,1)S(1)}, bf16[80,1152]{1,0:T(8,128)(2,1)S(1)}, u32[]{:S(2)}, u32[]{:S(2)}) %collective-permute-start.1) | collective-permute-done | bytes 184352 | tf_op jit(solution)/shard_map/ppermute | solution.py:240
  17.1 3.3 %collective-permute-start.7 = (bf16[320,1152]{1,0:T(8,128)(2,1)S(1)}, bf16[320,1152]{1,0:T(8,128)(2,1)S(1)}, u32[]{:S(2)}, u32[]{:S(2)}) collective-permute-start(bf16[320,1152]{1,0:T(8,128)(2,1)S(1)} %shard_map.29.refs_3_), channel_id=1, source_target_pairs={{0,32},{1,33},{2,34},{3,35},{8,10},{9,11},{10,8},{11,9},{16,48},{1... | collective-permute-start | bytes 2211848 | tf_op jit(solution)/shard_map/ppermute | solution.py:240
  20.4 1.1 %collective-permute-start.6 = (bf16[320,1152]{1,0:T(8,128)(2,1)S(1)}, bf16[320,1152]{1,0:T(8,128)(2,1)S(1)}, u32[]{:S(2)}, u32[]{:S(2)}) collective-permute-start(bf16[320,1152]{1,0:T(8,128)(2,1)S(1)} %shard_map.29.refs_3_), channel_id=1, source_target_pairs={{0,48},{1,49},{2,50},{3,51},{8,11},{9,8},{10,9},{11,10},{16,0},{17... | collective-permute-start | bytes 2211848 | tf_op jit(solution)/shard_map/ppermute | solution.py:240
  21.4 1.0 %collective-permute-start.5 = (bf16[320,1152]{1,0:T(8,128)(2,1)S(1)}, bf16[320,1152]{1,0:T(8,128)(2,1)S(1)}, u32[]{:S(2)}, u32[]{:S(2)}) collective-permute-start(bf16[320,1152]{1,0:T(8,128)(2,1)S(1)} %shard_map.29.refs_3_), channel_id=1, source_target_pairs={{0,16},{1,17},{2,18},{3,19},{8,9},{9,10},{10,11},{11,8},{16,32},{1... | collective-permute-start | bytes 2211848 | tf_op jit(solution)/shard_map/ppermute | solution.py:240
  22.4 3.2 %collective-permute-start.11 = (bf16[80,1152]{1,0:T(8,128)(2,1)S(1)}, bf16[80,1152]{1,0:T(8,128)(2,1)S(1)}, u32[]{:S(2)}, u32[]{:S(2)}) collective-permute-start(bf16[80,1152]{1,0:T(8,128)(2,1)S(1)} %collective-permute-done.10.refs_5_), channel_id=1, source_target_pairs={{0,196},{4,0},{64,4},{68,64},{128,68},{132,128},{192,132},{196,192... | collective-permute-start | bytes 552968 | tf_op jit(solution)/shard_map/ppermute | solution.py:228
  25.6 3.1 %collective-permute-done.11.refs_6_ = bf16[80,1152]{1,0:T(8,128)(2,1)S(1)} collective-permute-done((bf16[80,1152]{1,0:T(8,128)(2,1)S(1)}, bf16[80,1152]{1,0:T(8,128)(2,1)S(1)}, u32[]{:S(2)}, u32[]{:S(2)}) %collective-permute-start.11) | collective-permute-done | bytes 184352 | tf_op jit(solution)/shard_map/ppermute | solution.py:228
  28.7 3.7 %collective-permute-done.9.refs_3_ = bf16[80,1152]{1,0:T(8,128)(2,1)S(1)} collective-permute-done((bf16[80,1152]{1,0:T(8,128)(2,1)S(1)}, bf16[80,1152]{1,0:T(8,128)(2,1)S(1)}, u32[]{:S(2)}, u32[]{:S(2)}) %collective-permute-start.9) | collective-permute-done | bytes 184352 | tf_op jit(solution)/shard_map/ppermute | solution.py:228
  32.4 0.1 shard_map.34.block_ref.refs_4_
  32.6 0.4 shard_map.35
  33.1 5.3 %collective-permute-done.6.refs_1_ = bf16[320,1152]{1,0:T(8,128)(2,1)S(1)} collective-permute-done((bf16[320,1152]{1,0:T(8,128)(2,1)S(1)}, bf16[320,1152]{1,0:T(8,128)(2,1)S(1)}, u32[]{:S(2)}, u32[]{:S(2)}) %collective-permute-start.6) | collective-permute-done | bytes 737312 | tf_op jit(solution)/shard_map/ppermute | solution.py:240
  38.4 0.4 shard_map.36
  38.8 2.5 %collective-permute-done.13.refs_0_ = bf16[80,1152]{1,0:T(8,128)(2,1)S(1)} collective-permute-done((bf16[80,1152]{1,0:T(8,128)(2,1)S(1)}, bf16[80,1152]{1,0:T(8,128)(2,1)S(1)}, u32[]{:S(2)}, u32[]{:S(2)}) %collective-permute-start.13) | collective-permute-done | bytes 184352 | tf_op jit(solution)/shard_map/ppermute | solution.py:228
  41.3 0.3 collective-permute-start.14
  41.6 0.2 shard_map.38
  41.8 1.2 %collective-permute-done.14.block_ref.refs_7_ = bf16[80,1152]{1,0:T(8,128)(2,1)S(1)} collective-permute-done((bf16[80,1152]{1,0:T(8,128)(2,1)S(1)}, bf16[80,1152]{1,0:T(8,128)(2,1)S(1)}, u32[]{:S(2)}, u32[]{:S(2)}) %collective-permute-start.14) | collective-permute-done | bytes 184352 | tf_op jit(solution)/shard_map/ppermute | solution.py:228
  43.0 0.2 shard_map.39
  43.2 4.6 %shard_map.40 = (bf16[320,1280]{1,0:T(8,128)(2,1)S(1)}, bf16[320,1280]{1,0:T(8,128)(2,1)S(1)}, bf16[320,1280]{1,0:T(8,128)(2,1)S(1)}, bf16[320,1280]{1,0:T(8,128)(2,1)S(1)}, f32[2,1024]{1,0:T(2,128)S(1)}) custom-call(bf16[320,1152]{1,0:T(8,128)(2,1)S(1)} %get-tuple-element.47.refs_0_, bf16[320,1152]{1,0:T(8,128)(2,1)S(1)} %get-tuple-element.48.refs_1_, ...), custom_call_target="tpu_custom_call" | custom-call | tf_op jit(solution)/shard_map/pallas_call | solution.py:31
  47.8 1.0 %shard_map.42.refs_2_ = bf16[320,1024]{1,0:T(8,128)(2,1)S(1)} custom-call(bf16[320,1280]{1,0:T(8,128)(2,1)S(1)} %get-tuple-element.63.kernel_ref, bf16[560,1024]{1,0:T(8,128)(2,1)S(1)} %get-tuple-element.50.refs_1_.refs_0_, bf16[560,1024]{1,0:T(8,128)(2,1)S(1)} %get-tuple-element.51.refs_2_.refs_1_, bf16[80,1024]{1,0:T(8,128)(2,1)S(1)} %get-tuple-element.61.refs_2_, ...), custom_call_target="tpu_custom_call" | custom-call | tf_op jit(solution)/shard_map/pallas_call | solution.py:31
  48.9 2.4 %collective-permute-start.15 = (bf16[320,1024]{1,0:T(8,128)(2,1)S(1)}, bf16[320,1024]{1,0:T(8,128)(2,1)S(1)}, u32[]{:S(2)}, u32[]{:S(2)}) collective-permute-start(bf16[320,1024]{1,0:T(8,128)(2,1)S(1)} %shard_map.42.refs_2_), channel_id=1, source_target_pairs={{0,48},{1,49},{2,50},{3,51},{8,11},{9,8},{10,9},{11,10},{16,0},{17... | collective-permute-start | bytes 1966088 | tf_op jit(solution)/shard_map/ppermute | solution.py:240
  51.2 1.0 %shard_map.43.refs_3_ = bf16[320,1024]{1,0:T(8,128)(2,1)S(1)} custom-call(bf16[320,1280]{1,0:T(8,128)(2,1)S(1)} %get-tuple-element.64.kernel_ref, bf16[560,1024]{1,0:T(8,128)(2,1)S(1)} %get-tuple-element.50.refs_1_.refs_0_, bf16[560,1024]{1,0:T(8,128)(2,1)S(1)} %get-tuple-element.51.refs_2_.refs_1_, bf16[80,1024]{1,0:T(8,128)(2,1)S(1)} %get-tuple-element.61.refs_2_, ...), custom_call_target="tpu_custom_call" | custom-call | tf_op jit(solution)/shard_map/pallas_call | solution.py:31
  52.4 2.5 %collective-permute-done.18.refs_1_ = f32[2,1024]{1,0:T(2,128)S(1)} collective-permute-done((f32[2,1024]{1,0:T(2,128)S(1)}, f32[2,1024]{1,0:T(2,128)S(1)}, u32[]{:S(2)}, u32[]{:S(2)}) %collective-permute-start.18) | collective-permute-done | bytes 8224 | tf_op jit(solution)/shard_map/ppermute | solution.py:228
  54.9 1.4 %collective-permute-start.21 = (f32[2,1024]{1,0:T(2,128)S(1)}, f32[2,1024]{1,0:T(2,128)S(1)}, u32[]{:S(2)}, u32[]{:S(2)}) collective-permute-start(f32[2,1024]{1,0:T(2,128)S(1)} %shard_map.45.refs_0_), channel_id=1, source_target_pairs={{0,128},{4,132},{64,192},{68,196},{128,0},{132,4},{192,64},{196,68... | collective-permute-start | bytes 24584 | tf_op jit(solution)/shard_map/ppermute | solution.py:228
  56.3 0.6 collective-permute-start.20
  56.9 2.3 %collective-permute-start.19 = (f32[2,1024]{1,0:T(2,128)S(1)}, f32[2,1024]{1,0:T(2,128)S(1)}, u32[]{:S(2)}, u32[]{:S(2)}) collective-permute-start(f32[2,1024]{1,0:T(2,128)S(1)} %shard_map.45.refs_0_), channel_id=1, source_target_pairs={{0,64},{4,68},{64,128},{68,132},{128,192},{132,196},{192,0},{196,4... | collective-permute-start | bytes 24584 | tf_op jit(solution)/shard_map/ppermute | solution.py:228
  59.2 1.0 %shard_map.44.refs_4_ = bf16[320,1024]{1,0:T(8,128)(2,1)S(1)} custom-call(bf16[320,1280]{1,0:T(8,128)(2,1)S(1)} %get-tuple-element.65.kernel_ref, bf16[560,1024]{1,0:T(8,128)(2,1)S(1)} %get-tuple-element.50.refs_1_.refs_0_, bf16[560,1024]{1,0:T(8,128)(2,1)S(1)} %get-tuple-element.51.refs_2_.refs_1_, bf16[80,1024]{1,0:T(8,128)(2,1)S(1)} %get-tuple-element.61.refs_2_, ...), custom_call_target="tpu_custom_call" | custom-call | tf_op jit(solution)/shard_map/pallas_call | solution.py:31
  60.3 2.2 %collective-permute-done.21.refs_3_ = f32[2,1024]{1,0:T(2,128)S(1)} collective-permute-done((f32[2,1024]{1,0:T(2,128)S(1)}, f32[2,1024]{1,0:T(2,128)S(1)}, u32[]{:S(2)}, u32[]{:S(2)}) %collective-permute-start.21) | collective-permute-done | bytes 8224 | tf_op jit(solution)/shard_map/ppermute | solution.py:228
  62.5 0.5 collective-permute-start.17
  63.0 1.2 %collective-permute-done.22.refs_1_ = f32[2,1024]{1,0:T(2,128)S(1)} collective-permute-done((f32[2,1024]{1,0:T(2,128)S(1)}, f32[2,1024]{1,0:T(2,128)S(1)}, u32[]{:S(2)}, u32[]{:S(2)}) %collective-permute-start.22) | collective-permute-done | bytes 8224 | tf_op jit(solution)/shard_map/ppermute | solution.py:228
  64.2 3.1 %collective-permute-start.25 = (f32[2,1024]{1,0:T(2,128)S(1)}, f32[2,1024]{1,0:T(2,128)S(1)}, u32[]{:S(2)}, u32[]{:S(2)}) collective-permute-start(f32[2,1024]{1,0:T(2,128)S(1)} %shard_map.47.refs_0_), channel_id=1, source_target_pairs={{0,32},{1,33},{2,34},{3,35},{8,10},{9,11},{10,8},{11,9},{16,48},{1... | collective-permute-start | bytes 24584 | tf_op jit(solution)/shard_map/ppermute | solution.py:240
  67.3 0.7 collective-permute-start.24
  68.0 1.3 %collective-permute-start.23 = (f32[2,1024]{1,0:T(2,128)S(1)}, f32[2,1024]{1,0:T(2,128)S(1)}, u32[]{:S(2)}, u32[]{:S(2)}) collective-permute-start(f32[2,1024]{1,0:T(2,128)S(1)} %shard_map.47.refs_0_), channel_id=1, source_target_pairs={{0,16},{1,17},{2,18},{3,19},{8,9},{9,10},{10,11},{11,8},{16,32},{1... | collective-permute-start | bytes 24584 | tf_op jit(solution)/shard_map/ppermute | solution.py:240
  69.3 1.0 %shard_map.41.own_ref = f32[320,1024]{1,0:T(8,128)S(1)} custom-call(bf16[320,1280]{1,0:T(8,128)(2,1)S(1)} %get-tuple-element.60.kernel_ref, bf16[560,1024]{1,0:T(8,128)(2,1)S(1)} %get-tuple-element.50.refs_1_.refs_0_, bf16[560,1024]{1,0:T(8,128)(2,1)S(1)} %get-tuple-element.51.refs_2_.refs_1_, bf16[80,1024]{1,0:T(8,128)(2,1)S(1)} %get-tuple-element.61.refs_2_, ...), custom_call_target="tpu_custom_call" | custom-call | tf_op jit(solution)/shard_map/pallas_call | solution.py:31
  70.4 4.4 %collective-permute-done.25.refs_3_ = f32[2,1024]{1,0:T(2,128)S(1)} collective-permute-done((f32[2,1024]{1,0:T(2,128)S(1)}, f32[2,1024]{1,0:T(2,128)S(1)}, u32[]{:S(2)}, u32[]{:S(2)}) %collective-permute-start.25) | collective-permute-done | bytes 8224 | tf_op jit(solution)/shard_map/ppermute | solution.py:240
  74.7 0.3 shard_map.49
  75.0 0.9 %collective-permute-start.26 = (bf16[96,1024]{1,0:T(8,128)(2,1)S(1)}, bf16[96,1024]{1,0:T(8,128)(2,1)S(1)}, u32[]{:S(2)}, u32[]{:S(2)}) collective-permute-start(bf16[96,1024]{1,0:T(8,128)(2,1)S(1)} %get-tuple-element.68), channel_id=1, source_target_pairs={{0,3},{1,0},{2,1},{3,2},{8,56},{9,57},{10,58},{11,59},{16,19},{17,... | collective-permute-start | bytes 589832 | tf_op jit(solution)/shard_map/ppermute | solution.py:240
  75.9 2.4 %collective-permute-start.27 = (bf16[96,1024]{1,0:T(8,128)(2,1)S(1)}, bf16[96,1024]{1,0:T(8,128)(2,1)S(1)}, u32[]{:S(2)}, u32[]{:S(2)}) collective-permute-start(bf16[96,1024]{1,0:T(8,128)(2,1)S(1)} %get-tuple-element.69), channel_id=1, source_target_pairs={{0,1},{1,2},{2,3},{3,0},{8,24},{9,25},{10,26},{11,27},{16,17},{17,... | collective-permute-start | bytes 589832 | tf_op jit(solution)/shard_map/ppermute | solution.py:240
  78.4 0.6 collective-permute-start.28
  78.9 3.1 %collective-permute-done.26.refs_0_ = bf16[96,1024]{1,0:T(8,128)(2,1)S(1)} collective-permute-done((bf16[96,1024]{1,0:T(8,128)(2,1)S(1)}, bf16[96,1024]{1,0:T(8,128)(2,1)S(1)}, u32[]{:S(2)}, u32[]{:S(2)}) %collective-permute-start.26) | collective-permute-done | bytes 196640 | tf_op jit(solution)/shard_map/ppermute | solution.py:240
  82.0 1.7 %collective-permute-done.27.refs_1_ = bf16[96,1024]{1,0:T(8,128)(2,1)S(1)} collective-permute-done((bf16[96,1024]{1,0:T(8,128)(2,1)S(1)}, bf16[96,1024]{1,0:T(8,128)(2,1)S(1)}, u32[]{:S(2)}, u32[]{:S(2)}) %collective-permute-start.27) | collective-permute-done | bytes 196640 | tf_op jit(solution)/shard_map/ppermute | solution.py:240
  83.7 1.8 %collective-permute-done.28.refs_2_ = bf16[96,1024]{1,0:T(8,128)(2,1)S(1)} collective-permute-done((bf16[96,1024]{1,0:T(8,128)(2,1)S(1)}, bf16[96,1024]{1,0:T(8,128)(2,1)S(1)}, u32[]{:S(2)}, u32[]{:S(2)}) %collective-permute-start.28) | collective-permute-done | bytes 196640 | tf_op jit(solution)/shard_map/ppermute | solution.py:240
  85.5 0.9 %shard_map.50 = f32[80,1024]{1,0:T(8,128)} custom-call(f32[80,1024]{1,0:T(8,128)S(1)} %get-tuple-element.67.own_ref, bf16[80,1152]{1,0:T(8,128)(2,1)S(1)} %shard_map.28.refs_0_.packed_ref, f32[2,1024]{1,0:T(2,128)S(1)} %shard_map.48.sums_ref, bf16[96,1024]{1,0:T(8,128)(2,1)S(1)} %collective-permute-done.26.refs_0_, ...), custom_call_target="tpu_custom_call" | custom-call | tf_op jit(solution)/shard_map/pallas_call | solution.py:31
  (37 shorter events, 0.5 us)
Async XLA Ops:
  0.0 0.9 %copy-start = (bf16[80,1024]{1,0:T(8,128)(2,1)S(1)}, bf16[80,1024]{1,0:T(8,128)(2,1)}, u32[]{:S(2)}) copy-start(bf16[80,1024]{1,0:T(8,128)(2,1)} %clips_hbm.1) | copy-start | bytes 491524
  0.9 0.7 copy-start.1
  2.1 10.6 %collective-permute-start.4 = (bf16[80,1152]{1,0:T(8,128)(2,1)S(1)}, bf16[80,1152]{1,0:T(8,128)(2,1)S(1)}, u32[]{:S(2)}, u32[]{:S(2)}) collective-permute-start(bf16[80,1152]{1,0:T(8,128)(2,1)S(1)} %shard_map.28.refs_0_.packed_ref), channel_id=1, source_target_pairs={{0,196},{4,0},{64,4},{68,64},{128,68},{132,128},{192,132},{196,192... | collective-permute-start | bytes 552968 | tf_op jit(solution)/shard_map/ppermute | solution.py:228
  8.0 7.9 %collective-permute-start.3 = (bf16[80,1152]{1,0:T(8,128)(2,1)S(1)}, bf16[80,1152]{1,0:T(8,128)(2,1)S(1)}, u32[]{:S(2)}, u32[]{:S(2)}) collective-permute-start(bf16[80,1152]{1,0:T(8,128)(2,1)S(1)} %shard_map.28.refs_0_.packed_ref), channel_id=1, source_target_pairs={{0,4},{4,64},{64,68},{68,128},{128,132},{132,192},{192,196},{196,0... | collective-permute-start | bytes 552968 | tf_op jit(solution)/shard_map/ppermute | solution.py:228
  8.0 7.9 %collective-permute-start.2 = (bf16[80,1152]{1,0:T(8,128)(2,1)S(1)}, bf16[80,1152]{1,0:T(8,128)(2,1)S(1)}, u32[]{:S(2)}, u32[]{:S(2)}) collective-permute-start(bf16[80,1152]{1,0:T(8,128)(2,1)S(1)} %shard_map.28.refs_0_.packed_ref), channel_id=1, source_target_pairs={{0,2},{1,3},{2,0},{3,1},{8,40},{9,41},{10,42},{11,43},{16,18},{17,... | collective-permute-start | bytes 552968 | tf_op jit(solution)/shard_map/ppermute | solution.py:240
  9.4 7.6 %collective-permute-start.1 = (bf16[80,1152]{1,0:T(8,128)(2,1)S(1)}, bf16[80,1152]{1,0:T(8,128)(2,1)S(1)}, u32[]{:S(2)}, u32[]{:S(2)}) collective-permute-start(bf16[80,1152]{1,0:T(8,128)(2,1)S(1)} %shard_map.28.refs_0_.packed_ref), channel_id=1, source_target_pairs={{0,3},{1,0},{2,1},{3,2},{8,56},{9,57},{10,58},{11,59},{16,19},{17,... | collective-permute-start | bytes 552968 | tf_op jit(solution)/shard_map/ppermute | solution.py:240
  9.4 7.6 %collective-permute-start = (bf16[80,1152]{1,0:T(8,128)(2,1)S(1)}, bf16[80,1152]{1,0:T(8,128)(2,1)S(1)}, u32[]{:S(2)}, u32[]{:S(2)}) collective-permute-start(bf16[80,1152]{1,0:T(8,128)(2,1)S(1)} %shard_map.28.refs_0_.packed_ref), channel_id=1, source_target_pairs={{0,1},{1,2},{2,3},{3,0},{8,24},{9,25},{10,26},{11,27},{16,17},{17,... | collective-permute-start | bytes 552968 | tf_op jit(solution)/shard_map/ppermute | solution.py:240
  12.6 9.7 %collective-permute-start.10 = (bf16[80,1152]{1,0:T(8,128)(2,1)S(1)}, bf16[80,1152]{1,0:T(8,128)(2,1)S(1)}, u32[]{:S(2)}, u32[]{:S(2)}) collective-permute-start(bf16[80,1152]{1,0:T(8,128)(2,1)S(1)} %collective-permute-done.4.refs_5_.refs_4_), channel_id=1, source_target_pairs={{0,196},{4,0},{64,4},{68,64},{128,68},{132,128},{192,132},{196,192... | collective-permute-start | bytes 552968 | tf_op jit(solution)/shard_map/ppermute | solution.py:228
  15.9 9.7 %collective-permute-start.8 = (bf16[80,1152]{1,0:T(8,128)(2,1)S(1)}, bf16[80,1152]{1,0:T(8,128)(2,1)S(1)}, u32[]{:S(2)}, u32[]{:S(2)}) collective-permute-start(bf16[80,1152]{1,0:T(8,128)(2,1)S(1)} %collective-permute-done.3.refs_4_.refs_1_), channel_id=1, source_target_pairs={{0,4},{4,64},{64,68},{68,128},{128,132},{132,192},{192,196},{196,0... | collective-permute-start | bytes 552968 | tf_op jit(solution)/shard_map/ppermute | solution.py:228
  17.1 16.0 %collective-permute-start.7 = (bf16[320,1152]{1,0:T(8,128)(2,1)S(1)}, bf16[320,1152]{1,0:T(8,128)(2,1)S(1)}, u32[]{:S(2)}, u32[]{:S(2)}) collective-permute-start(bf16[320,1152]{1,0:T(8,128)(2,1)S(1)} %shard_map.29.refs_3_), channel_id=1, source_target_pairs={{0,32},{1,33},{2,34},{3,35},{8,10},{9,11},{10,8},{11,9},{16,48},{1... | collective-permute-start | bytes 2211848 | tf_op jit(solution)/shard_map/ppermute | solution.py:240
  20.4 18.1 %collective-permute-start.6 = (bf16[320,1152]{1,0:T(8,128)(2,1)S(1)}, bf16[320,1152]{1,0:T(8,128)(2,1)S(1)}, u32[]{:S(2)}, u32[]{:S(2)}) collective-permute-start(bf16[320,1152]{1,0:T(8,128)(2,1)S(1)} %shard_map.29.refs_3_), channel_id=1, source_target_pairs={{0,48},{1,49},{2,50},{3,51},{8,11},{9,8},{10,9},{11,10},{16,0},{17... | collective-permute-start | bytes 2211848 | tf_op jit(solution)/shard_map/ppermute | solution.py:240
  21.4 17.0 %collective-permute-start.5 = (bf16[320,1152]{1,0:T(8,128)(2,1)S(1)}, bf16[320,1152]{1,0:T(8,128)(2,1)S(1)}, u32[]{:S(2)}, u32[]{:S(2)}) collective-permute-start(bf16[320,1152]{1,0:T(8,128)(2,1)S(1)} %shard_map.29.refs_3_), channel_id=1, source_target_pairs={{0,16},{1,17},{2,18},{3,19},{8,9},{9,10},{10,11},{11,8},{16,32},{1... | collective-permute-start | bytes 2211848 | tf_op jit(solution)/shard_map/ppermute | solution.py:240
  22.4 6.3 %collective-permute-start.11 = (bf16[80,1152]{1,0:T(8,128)(2,1)S(1)}, bf16[80,1152]{1,0:T(8,128)(2,1)S(1)}, u32[]{:S(2)}, u32[]{:S(2)}) collective-permute-start(bf16[80,1152]{1,0:T(8,128)(2,1)S(1)} %collective-permute-done.10.refs_5_), channel_id=1, source_target_pairs={{0,196},{4,0},{64,4},{68,64},{128,68},{132,128},{192,132},{196,192... | collective-permute-start | bytes 552968 | tf_op jit(solution)/shard_map/ppermute | solution.py:228
  25.6 6.7 %collective-permute-start.9 = (bf16[80,1152]{1,0:T(8,128)(2,1)S(1)}, bf16[80,1152]{1,0:T(8,128)(2,1)S(1)}, u32[]{:S(2)}, u32[]{:S(2)}) collective-permute-start(bf16[80,1152]{1,0:T(8,128)(2,1)S(1)} %collective-permute-done.8.refs_2_), channel_id=1, source_target_pairs={{0,4},{4,64},{64,68},{68,128},{128,132},{132,192},{192,196},{196,0... | collective-permute-start | bytes 552968 | tf_op jit(solution)/shard_map/ppermute | solution.py:228
  32.5 6.0 %collective-permute-start.12 = (bf16[560,1152]{1,0:T(8,128)(2,1)S(1)}, bf16[560,1152]{1,0:T(8,128)(2,1)S(1)}, u32[]{:S(2)}, u32[]{:S(2)}) collective-permute-start(bf16[560,1152]{1,0:T(8,128)(2,1)S(1)} %shard_map.34.block_ref.refs_4_), channel_id=1, source_target_pairs={{0,8},{8,0},{1,9},{9,1},{2,10},{10,2},{3,11},{11,3},{4,12},{12,4},... | collective-permute-start | bytes 3870728 | tf_op jit(solution)/shard_map/ppermute | solution.py:228
  33.0 8.3 %collective-permute-start.13 = (bf16[80,1152]{1,0:T(8,128)(2,1)S(1)}, bf16[80,1152]{1,0:T(8,128)(2,1)S(1)}, u32[]{:S(2)}, u32[]{:S(2)}) collective-permute-start(bf16[80,1152]{1,0:T(8,128)(2,1)S(1)} %collective-permute-done.9.refs_3_), channel_id=1, source_target_pairs={{0,4},{4,64},{64,68},{68,128},{128,132},{132,192},{192,196},{196,0... | collective-permute-start | bytes 552968 | tf_op jit(solution)/shard_map/ppermute | solution.py:228
  41.3 1.7 %collective-permute-start.14 = (bf16[80,1152]{1,0:T(8,128)(2,1)S(1)}, bf16[80,1152]{1,0:T(8,128)(2,1)S(1)}, u32[]{:S(2)}, u32[]{:S(2)}) collective-permute-start(bf16[80,1152]{1,0:T(8,128)(2,1)S(1)} %shard_map.37.block_ref.refs_6_), channel_id=1, source_target_pairs={{0,8},{8,0},{1,9},{9,1},{2,10},{10,2},{3,11},{11,3},{4,12},{12,4},... | collective-permute-start | bytes 552968 | tf_op jit(solution)/shard_map/ppermute | solution.py:228
  48.9 15.3 %collective-permute-start.15 = (bf16[320,1024]{1,0:T(8,128)(2,1)S(1)}, bf16[320,1024]{1,0:T(8,128)(2,1)S(1)}, u32[]{:S(2)}, u32[]{:S(2)}) collective-permute-start(bf16[320,1024]{1,0:T(8,128)(2,1)S(1)} %shard_map.42.refs_2_), channel_id=1, source_target_pairs={{0,48},{1,49},{2,50},{3,51},{8,11},{9,8},{10,9},{11,10},{16,0},{17... | collective-permute-start | bytes 1966088 | tf_op jit(solution)/shard_map/ppermute | solution.py:240
  51.2 3.7 %collective-permute-start.18 = (f32[2,1024]{1,0:T(2,128)S(1)}, f32[2,1024]{1,0:T(2,128)S(1)}, u32[]{:S(2)}, u32[]{:S(2)}) collective-permute-start(f32[2,1024]{1,0:T(2,128)S(1)} %get-tuple-element.66.refs_0_), channel_id=1, source_target_pairs={{0,4},{4,0},{64,68},{68,64},{128,132},{132,128},{192,196},{196,192... | collective-permute-start | bytes 24584 | tf_op jit(solution)/shard_map/ppermute | solution.py:228
  52.3 18.1 %collective-permute-start.16 = (bf16[320,1024]{1,0:T(8,128)(2,1)S(1)}, bf16[320,1024]{1,0:T(8,128)(2,1)S(1)}, u32[]{:S(2)}, u32[]{:S(2)}) collective-permute-start(bf16[320,1024]{1,0:T(8,128)(2,1)S(1)} %shard_map.43.refs_3_), channel_id=1, source_target_pairs={{0,16},{1,17},{2,18},{3,19},{8,9},{9,10},{10,11},{11,8},{16,32},{1... | collective-permute-start | bytes 1966088 | tf_op jit(solution)/shard_map/ppermute | solution.py:240
  54.9 7.6 %collective-permute-start.21 = (f32[2,1024]{1,0:T(2,128)S(1)}, f32[2,1024]{1,0:T(2,128)S(1)}, u32[]{:S(2)}, u32[]{:S(2)}) collective-permute-start(f32[2,1024]{1,0:T(2,128)S(1)} %shard_map.45.refs_0_), channel_id=1, source_target_pairs={{0,128},{4,132},{64,192},{68,196},{128,0},{132,4},{192,64},{196,68... | collective-permute-start | bytes 24584 | tf_op jit(solution)/shard_map/ppermute | solution.py:228
  56.3 6.6 %collective-permute-start.20 = (f32[2,1024]{1,0:T(2,128)S(1)}, f32[2,1024]{1,0:T(2,128)S(1)}, u32[]{:S(2)}, u32[]{:S(2)}) collective-permute-start(f32[2,1024]{1,0:T(2,128)S(1)} %shard_map.45.refs_0_), channel_id=1, source_target_pairs={{0,192},{4,196},{64,0},{68,4},{128,64},{132,68},{192,128},{196,132... | collective-permute-start | bytes 24584 | tf_op jit(solution)/shard_map/ppermute | solution.py:228
  56.9 6.1 %collective-permute-start.19 = (f32[2,1024]{1,0:T(2,128)S(1)}, f32[2,1024]{1,0:T(2,128)S(1)}, u32[]{:S(2)}, u32[]{:S(2)}) collective-permute-start(f32[2,1024]{1,0:T(2,128)S(1)} %shard_map.45.refs_0_), channel_id=1, source_target_pairs={{0,64},{4,68},{64,128},{68,132},{128,192},{132,196},{192,0},{196,4... | collective-permute-start | bytes 24584 | tf_op jit(solution)/shard_map/ppermute | solution.py:228
  62.5 12.3 %collective-permute-start.17 = (bf16[320,1024]{1,0:T(8,128)(2,1)S(1)}, bf16[320,1024]{1,0:T(8,128)(2,1)S(1)}, u32[]{:S(2)}, u32[]{:S(2)}) collective-permute-start(bf16[320,1024]{1,0:T(8,128)(2,1)S(1)} %shard_map.44.refs_4_), channel_id=1, source_target_pairs={{0,32},{1,33},{2,34},{3,35},{8,10},{9,11},{10,8},{11,9},{16,48},{1... | collective-permute-start | bytes 1966088 | tf_op jit(solution)/shard_map/ppermute | solution.py:240
  63.0 1.2 %collective-permute-start.22 = (f32[2,1024]{1,0:T(2,128)S(1)}, f32[2,1024]{1,0:T(2,128)S(1)}, u32[]{:S(2)}, u32[]{:S(2)}) collective-permute-start(f32[2,1024]{1,0:T(2,128)S(1)} %shard_map.46.refs_0_), channel_id=1, source_target_pairs={{0,8},{8,0},{1,9},{9,1},{2,10},{10,2},{3,11},{11,3},{4,12},{12,4},... | collective-permute-start | bytes 24584 | tf_op jit(solution)/shard_map/ppermute | solution.py:228
  64.2 10.5 %collective-permute-start.25 = (f32[2,1024]{1,0:T(2,128)S(1)}, f32[2,1024]{1,0:T(2,128)S(1)}, u32[]{:S(2)}, u32[]{:S(2)}) collective-permute-start(f32[2,1024]{1,0:T(2,128)S(1)} %shard_map.47.refs_0_), channel_id=1, source_target_pairs={{0,32},{1,33},{2,34},{3,35},{8,10},{9,11},{10,8},{11,9},{16,48},{1... | collective-permute-start | bytes 24584 | tf_op jit(solution)/shard_map/ppermute | solution.py:240
  67.3 7.5 %collective-permute-start.24 = (f32[2,1024]{1,0:T(2,128)S(1)}, f32[2,1024]{1,0:T(2,128)S(1)}, u32[]{:S(2)}, u32[]{:S(2)}) collective-permute-start(f32[2,1024]{1,0:T(2,128)S(1)} %shard_map.47.refs_0_), channel_id=1, source_target_pairs={{0,48},{1,49},{2,50},{3,51},{8,11},{9,8},{10,9},{11,10},{16,0},{17... | collective-permute-start | bytes 24584 | tf_op jit(solution)/shard_map/ppermute | solution.py:240
  68.0 6.7 %collective-permute-start.23 = (f32[2,1024]{1,0:T(2,128)S(1)}, f32[2,1024]{1,0:T(2,128)S(1)}, u32[]{:S(2)}, u32[]{:S(2)}) collective-permute-start(f32[2,1024]{1,0:T(2,128)S(1)} %shard_map.47.refs_0_), channel_id=1, source_target_pairs={{0,16},{1,17},{2,18},{3,19},{8,9},{9,10},{10,11},{11,8},{16,32},{1... | collective-permute-start | bytes 24584 | tf_op jit(solution)/shard_map/ppermute | solution.py:240
  75.0 7.0 %collective-permute-start.26 = (bf16[96,1024]{1,0:T(8,128)(2,1)S(1)}, bf16[96,1024]{1,0:T(8,128)(2,1)S(1)}, u32[]{:S(2)}, u32[]{:S(2)}) collective-permute-start(bf16[96,1024]{1,0:T(8,128)(2,1)S(1)} %get-tuple-element.68), channel_id=1, source_target_pairs={{0,3},{1,0},{2,1},{3,2},{8,56},{9,57},{10,58},{11,59},{16,19},{17,... | collective-permute-start | bytes 589832 | tf_op jit(solution)/shard_map/ppermute | solution.py:240
  75.9 7.7 %collective-permute-start.27 = (bf16[96,1024]{1,0:T(8,128)(2,1)S(1)}, bf16[96,1024]{1,0:T(8,128)(2,1)S(1)}, u32[]{:S(2)}, u32[]{:S(2)}) collective-permute-start(bf16[96,1024]{1,0:T(8,128)(2,1)S(1)} %get-tuple-element.69), channel_id=1, source_target_pairs={{0,1},{1,2},{2,3},{3,0},{8,24},{9,25},{10,26},{11,27},{16,17},{17,... | collective-permute-start | bytes 589832 | tf_op jit(solution)/shard_map/ppermute | solution.py:240
  78.4 7.2 %collective-permute-start.28 = (bf16[96,1024]{1,0:T(8,128)(2,1)S(1)}, bf16[96,1024]{1,0:T(8,128)(2,1)S(1)}, u32[]{:S(2)}, u32[]{:S(2)}) collective-permute-start(bf16[96,1024]{1,0:T(8,128)(2,1)S(1)} %get-tuple-element.70), channel_id=1, source_target_pairs={{0,2},{1,3},{2,0},{3,1},{8,40},{9,41},{10,42},{11,43},{16,18},{17,... | collective-permute-start | bytes 589832 | tf_op jit(solution)/shard_map/ppermute | solution.py:240

commit v2 on v1

--- a/solution.py
+++ b/solution.py
@@ -262,12 +262,12 @@
     down.append(shift(down[1], Z, -1))
     up.append(shift(up[2], Z, 1))
     down.append(shift(down[2], Z, -1))
-    up.append(shift(up[3], Z, 1))
+    up.append(shift(down[3], Z, -1))
 
     blocks = [join([own, *up[1:4], *down[1:4]])]
     blocks += [shift(block, "core", 1) for block in blocks]
     early = [prep(block) for block in blocks]
-    blocks.append(join([up[4]], after=[member for member, _, _ in early]))
+    blocks.append(join([up[4]], after=[member for member, _, _ in early], flops=0))
     blocks.append(shift(blocks[-1], "core", 1))
     members, lines, counts = zip(*early, *[prep(block) for block in blocks[2:]])
 
@@ -276,9 +276,10 @@
     *kernel, sums = kernels([*rows, four], blocks, lines, counts)
     terms = [main(part, BF16, members) for part in kernel[:3]]
     received = [plane_shift(term, 2, -step) for step, term in zip(steps, terms)]
-    sums = plus([sums, shift(sums, Z, 1, flip=True)], after=terms[:2], flops=LONG)
-    others = [shift(sums, Z, step) for step in (2, -2, 4)]
-    sums = plus([sums, *others], after=terms[2:], flops=LONG)
+    below, above = shift(sums, Z, 1), shift(sums, Z, -1)
+    two = plus([sums, below], flops=0)
+    sums = plus([sums, below, above], after=terms[:2], flops=LONG)
+    sums = plus([sums, shift(sums, Z, 3), shift(two, Z, -3)], after=terms[2:], flops=LONG)
     sums = plus([sums, shift(sums, "core", 1)], after=received[:1], flops=LONG)
     others = [plane_shift(sums, 2, step) for step in steps]
     sums = plus([sums, *others], after=received[1:2], flops=LONG)

time: 86.6 us -> 85.2 us (0.984)
  waiting for transfers between devices: 33.8 us -> 30.3 us
  starting transfers between devices: 39.1 us -> 41.2 us
    ppermute x14, waiting for transfers between devices: 16.4 us -> 12.3 us  [shift(): return lax.ppermute(value, axis, pairs)]
    ppermute x14, starting transfers between devices: 17.2 us -> 19.9 us  [shift(): return lax.ppermute(value, axis, pairs)]
    pallas_call x18 -> x19, Pallas kernels: 11.4 us -> 11.4 us  [call(): pl.pallas_call(body, out_shape=outs, compiler_params=pltpu.CompilerParams...]
where the time goes in v2:
time: 85.2 us; the launch traced here: 85.1 us
  starting transfers between devices  41.2 us (48%)
  waiting for transfers between devices  30.3 us (36%)
  Pallas kernels  11.9 us (14%)
  local copies, waits for them, and re-layouts  1.57 us (2%)
    ppermute x15, starting transfers between devices, plane_shift(): return lax.ppermute(value, PLANE, pairs)  21.3 us
    ppermute x14, starting transfers between devices, shift(): return lax.ppermute(value, axis, pairs)  19.9 us
    ppermute x15, waiting for transfers between devices, plane_shift(): return lax.ppermute(value, PLANE, pairs)  17.9 us
    ppermute x14, waiting for transfers between devices, shift(): return lax.ppermute(value, axis, pairs)  12.3 us
    pallas_call x19, Pallas kernels, call(): pl.pallas_call(body, out_shape=outs, compiler_params=pltpu.CompilerParams...  11.4 us
  transfers between devices with their start and end apart: 29, of which 14 were waited for; matrix products, arithmetic and copies ran while one was open for 0% of the time, Pallas kernels for 5%

profile of v2, /device:TPU:6, one launch (start us, length us, event | category | flops | bytes accessed | tf_op | source)
XLA Modules:
  0.0 85.1 jit_solution(5737433271182430011)
XLA Ops:
  0.0 0.9 %copy-done = bf16[80,1024]{1,0:T(8,128)(2,1)S(1)} copy-done((bf16[80,1024]{1,0:T(8,128)(2,1)S(1)}, bf16[80,1024]{1,0:T(8,128)(2,1)}, u32[]{:S(2)}) %copy-start) | copy-done | bytes 163864
  0.9 0.7 copy-done.1
  1.6 0.5 shard_map.28.refs_0_.packed_ref
  2.1 5.9 %collective-permute-start.4 = (bf16[80,1152]{1,0:T(8,128)(2,1)S(1)}, bf16[80,1152]{1,0:T(8,128)(2,1)S(1)}, u32[]{:S(2)}, u32[]{:S(2)}) collective-permute-start(bf16[80,1152]{1,0:T(8,128)(2,1)S(1)} %shard_map.28.refs_0_.packed_ref), channel_id=1, source_target_pairs={{0,196},{4,0},{64,4},{68,64},{128,68},{132,128},{192,132},{196,192... | collective-permute-start | bytes 552968 | tf_op jit(solution)/shard_map/ppermute | solution.py:228
  8.0 1.4 %collective-permute-start.2 = (bf16[80,1152]{1,0:T(8,128)(2,1)S(1)}, bf16[80,1152]{1,0:T(8,128)(2,1)S(1)}, u32[]{:S(2)}, u32[]{:S(2)}) collective-permute-start(bf16[80,1152]{1,0:T(8,128)(2,1)S(1)} %shard_map.28.refs_0_.packed_ref), channel_id=1, source_target_pairs={{0,2},{1,3},{2,0},{3,1},{8,40},{9,41},{10,42},{11,43},{16,18},{17,... | collective-permute-start | bytes 552968 | tf_op jit(solution)/shard_map/ppermute | solution.py:240
  9.4 3.2 %collective-permute-start = (bf16[80,1152]{1,0:T(8,128)(2,1)S(1)}, bf16[80,1152]{1,0:T(8,128)(2,1)S(1)}, u32[]{:S(2)}, u32[]{:S(2)}) collective-permute-start(bf16[80,1152]{1,0:T(8,128)(2,1)S(1)} %shard_map.28.refs_0_.packed_ref), channel_id=1, source_target_pairs={{0,1},{1,2},{2,3},{3,0},{8,24},{9,25},{10,26},{11,27},{16,17},{17,... | collective-permute-start | bytes 552968 | tf_op jit(solution)/shard_map/ppermute | solution.py:240
  12.6 3.2 %collective-permute-start.10 = (bf16[80,1152]{1,0:T(8,128)(2,1)S(1)}, bf16[80,1152]{1,0:T(8,128)(2,1)S(1)}, u32[]{:S(2)}, u32[]{:S(2)}) collective-permute-start(bf16[80,1152]{1,0:T(8,128)(2,1)S(1)} %collective-permute-done.4.refs_5_.refs_4_), channel_id=1, source_target_pairs={{0,196},{4,0},{64,4},{68,64},{128,68},{132,128},{192,132},{196,192... | collective-permute-start | bytes 552968 | tf_op jit(solution)/shard_map/ppermute | solution.py:228
  15.9 1.1 %collective-permute-done.1.refs_2_ = bf16[80,1152]{1,0:T(8,128)(2,1)S(1)} collective-permute-done((bf16[80,1152]{1,0:T(8,128)(2,1)S(1)}, bf16[80,1152]{1,0:T(8,128)(2,1)S(1)}, u32[]{:S(2)}, u32[]{:S(2)}) %collective-permute-start.1) | collective-permute-done | bytes 184352 | tf_op jit(solution)/shard_map/ppermute | solution.py:240
  17.1 3.3 %collective-permute-start.7 = (bf16[320,1152]{1,0:T(8,128)(2,1)S(1)}, bf16[320,1152]{1,0:T(8,128)(2,1)S(1)}, u32[]{:S(2)}, u32[]{:S(2)}) collective-permute-start(bf16[320,1152]{1,0:T(8,128)(2,1)S(1)} %shard_map.29.refs_3_), channel_id=1, source_target_pairs={{0,32},{1,33},{2,34},{3,35},{8,10},{9,11},{10,8},{11,9},{16,48},{1... | collective-permute-start | bytes 2211848 | tf_op jit(solution)/shard_map/ppermute | solution.py:240
  20.4 1.1 %collective-permute-start.6 = (bf16[320,1152]{1,0:T(8,128)(2,1)S(1)}, bf16[320,1152]{1,0:T(8,128)(2,1)S(1)}, u32[]{:S(2)}, u32[]{:S(2)}) collective-permute-start(bf16[320,1152]{1,0:T(8,128)(2,1)S(1)} %shard_map.29.refs_3_), channel_id=1, source_target_pairs={{0,48},{1,49},{2,50},{3,51},{8,11},{9,8},{10,9},{11,10},{16,0},{17... | collective-permute-start | bytes 2211848 | tf_op jit(solution)/shard_map/ppermute | solution.py:240
  21.4 1.0 %collective-permute-start.5 = (bf16[320,1152]{1,0:T(8,128)(2,1)S(1)}, bf16[320,1152]{1,0:T(8,128)(2,1)S(1)}, u32[]{:S(2)}, u32[]{:S(2)}) collective-permute-start(bf16[320,1152]{1,0:T(8,128)(2,1)S(1)} %shard_map.29.refs_3_), channel_id=1, source_target_pairs={{0,16},{1,17},{2,18},{3,19},{8,9},{9,10},{10,11},{11,8},{16,32},{1... | collective-permute-start | bytes 2211848 | tf_op jit(solution)/shard_map/ppermute | solution.py:240
  22.4 3.2 %collective-permute-start.11 = (bf16[80,1152]{1,0:T(8,128)(2,1)S(1)}, bf16[80,1152]{1,0:T(8,128)(2,1)S(1)}, u32[]{:S(2)}, u32[]{:S(2)}) collective-permute-start(bf16[80,1152]{1,0:T(8,128)(2,1)S(1)} %collective-permute-done.10.refs_5_), channel_id=1, source_target_pairs={{0,196},{4,0},{64,4},{68,64},{128,68},{132,128},{192,132},{196,192... | collective-permute-start | bytes 552968 | tf_op jit(solution)/shard_map/ppermute | solution.py:228
  25.6 3.1 %collective-permute-done.11.refs_6_ = bf16[80,1152]{1,0:T(8,128)(2,1)S(1)} collective-permute-done((bf16[80,1152]{1,0:T(8,128)(2,1)S(1)}, bf16[80,1152]{1,0:T(8,128)(2,1)S(1)}, u32[]{:S(2)}, u32[]{:S(2)}) %collective-permute-start.11) | collective-permute-done | bytes 184352 | tf_op jit(solution)/shard_map/ppermute | solution.py:228
  28.7 3.7 %collective-permute-done.9.refs_3_ = bf16[80,1152]{1,0:T(8,128)(2,1)S(1)} collective-permute-done((bf16[80,1152]{1,0:T(8,128)(2,1)S(1)}, bf16[80,1152]{1,0:T(8,128)(2,1)S(1)}, u32[]{:S(2)}, u32[]{:S(2)}) %collective-permute-start.9) | collective-permute-done | bytes 184352 | tf_op jit(solution)/shard_map/ppermute | solution.py:228
  32.4 0.1 shard_map.34.block_ref.refs_4_
  32.5 0.1 collective-permute-start.12
  32.6 0.4 shard_map.35
  33.1 5.3 %collective-permute-done.6.refs_1_ = bf16[320,1152]{1,0:T(8,128)(2,1)S(1)} collective-permute-done((bf16[320,1152]{1,0:T(8,128)(2,1)S(1)}, bf16[320,1152]{1,0:T(8,128)(2,1)S(1)}, u32[]{:S(2)}, u32[]{:S(2)}) %collective-permute-start.6) | collective-permute-done | bytes 737312 | tf_op jit(solution)/shard_map/ppermute | solution.py:240
  38.4 0.4 shard_map.36
  38.8 1.3 %collective-permute-done.13.refs_0_ = bf16[80,1152]{1,0:T(8,128)(2,1)S(1)} collective-permute-done((bf16[80,1152]{1,0:T(8,128)(2,1)S(1)}, bf16[80,1152]{1,0:T(8,128)(2,1)S(1)}, u32[]{:S(2)}, u32[]{:S(2)}) %collective-permute-start.13) | collective-permute-done | bytes 184352 | tf_op jit(solution)/shard_map/ppermute | solution.py:228
  40.1 0.3 collective-permute-start.14
  40.4 0.2 shard_map.38
  40.6 1.2 %collective-permute-done.14.block_ref.refs_7_ = bf16[80,1152]{1,0:T(8,128)(2,1)S(1)} collective-permute-done((bf16[80,1152]{1,0:T(8,128)(2,1)S(1)}, bf16[80,1152]{1,0:T(8,128)(2,1)S(1)}, u32[]{:S(2)}, u32[]{:S(2)}) %collective-permute-start.14) | collective-permute-done | bytes 184352 | tf_op jit(solution)/shard_map/ppermute | solution.py:228
  41.8 0.2 shard_map.39
  42.0 4.6 %shard_map.40 = (bf16[320,1280]{1,0:T(8,128)(2,1)S(1)}, bf16[320,1280]{1,0:T(8,128)(2,1)S(1)}, bf16[320,1280]{1,0:T(8,128)(2,1)S(1)}, bf16[320,1280]{1,0:T(8,128)(2,1)S(1)}, f32[2,1024]{1,0:T(2,128)S(1)}) custom-call(bf16[320,1152]{1,0:T(8,128)(2,1)S(1)} %get-tuple-element.47.refs_0_, bf16[320,1152]{1,0:T(8,128)(2,1)S(1)} %get-tuple-element.48.refs_1_, ...), custom_call_target="tpu_custom_call" | custom-call | tf_op jit(solution)/shard_map/pallas_call | solution.py:31
  46.6 1.0 %shard_map.42.refs_3_ = bf16[320,1024]{1,0:T(8,128)(2,1)S(1)} custom-call(bf16[320,1280]{1,0:T(8,128)(2,1)S(1)} %get-tuple-element.63.kernel_ref, bf16[560,1024]{1,0:T(8,128)(2,1)S(1)} %get-tuple-element.50.refs_1_.refs_0_, bf16[560,1024]{1,0:T(8,128)(2,1)S(1)} %get-tuple-element.51.refs_2_.refs_1_, bf16[80,1024]{1,0:T(8,128)(2,1)S(1)} %get-tuple-element.61.refs_2_, ...), custom_call_target="tpu_custom_call" | custom-call | tf_op jit(solution)/shard_map/pallas_call | solution.py:31
  47.7 2.3 %collective-permute-start.15 = (bf16[320,1024]{1,0:T(8,128)(2,1)S(1)}, bf16[320,1024]{1,0:T(8,128)(2,1)S(1)}, u32[]{:S(2)}, u32[]{:S(2)}) collective-permute-start(bf16[320,1024]{1,0:T(8,128)(2,1)S(1)} %shard_map.42.refs_3_), channel_id=1, source_target_pairs={{0,48},{1,49},{2,50},{3,51},{8,11},{9,8},{10,9},{11,10},{16,0},{17... | collective-permute-start | bytes 1966088 | tf_op jit(solution)/shard_map/ppermute | solution.py:240
  50.0 3.2 %collective-permute-start.19 = (f32[2,1024]{1,0:T(2,128)S(1)}, f32[2,1024]{1,0:T(2,128)S(1)}, u32[]{:S(2)}, u32[]{:S(2)}) collective-permute-start(f32[2,1024]{1,0:T(2,128)S(1)} %get-tuple-element.66.refs_0_), channel_id=1, source_target_pairs={{0,196},{4,0},{64,4},{68,64},{128,68},{132,128},{192,132},{196,192... | collective-permute-start | bytes 24584 | tf_op jit(solution)/shard_map/ppermute | solution.py:228
  53.2 1.0 %shard_map.43.refs_4_ = bf16[320,1024]{1,0:T(8,128)(2,1)S(1)} custom-call(bf16[320,1280]{1,0:T(8,128)(2,1)S(1)} %get-tuple-element.64.kernel_ref, bf16[560,1024]{1,0:T(8,128)(2,1)S(1)} %get-tuple-element.50.refs_1_.refs_0_, bf16[560,1024]{1,0:T(8,128)(2,1)S(1)} %get-tuple-element.51.refs_2_.refs_1_, bf16[80,1024]{1,0:T(8,128)(2,1)S(1)} %get-tuple-element.61.refs_2_, ...), custom_call_target="tpu_custom_call" | custom-call | tf_op jit(solution)/shard_map/pallas_call | solution.py:31
  54.4 0.5 collective-permute-done.18.refs_1_
  54.9 0.8 collective-permute-start.21
  55.7 3.0 %collective-permute-start.20 = (f32[2,1024]{1,0:T(2,128)S(1)}, f32[2,1024]{1,0:T(2,128)S(1)}, u32[]{:S(2)}, u32[]{:S(2)}) collective-permute-start(f32[2,1024]{1,0:T(2,128)S(1)} %shard_map.45.refs_0_), channel_id=1, source_target_pairs={{0,68},{4,128},{64,132},{68,192},{128,196},{132,0},{192,4},{196,64... | collective-permute-start | bytes 24584 | tf_op jit(solution)/shard_map/ppermute | solution.py:228
  58.7 1.0 %shard_map.44.refs_3_ = bf16[320,1024]{1,0:T(8,128)(2,1)S(1)} custom-call(bf16[320,1280]{1,0:T(8,128)(2,1)S(1)} %get-tuple-element.65.kernel_ref, bf16[560,1024]{1,0:T(8,128)(2,1)S(1)} %get-tuple-element.50.refs_1_.refs_0_, bf16[560,1024]{1,0:T(8,128)(2,1)S(1)} %get-tuple-element.51.refs_2_.refs_1_, bf16[80,1024]{1,0:T(8,128)(2,1)S(1)} %get-tuple-element.61.refs_2_, ...), custom_call_target="tpu_custom_call" | custom-call | tf_op jit(solution)/shard_map/pallas_call | solution.py:31
  59.8 1.1 %collective-permute-start.17 = (bf16[320,1024]{1,0:T(8,128)(2,1)S(1)}, bf16[320,1024]{1,0:T(8,128)(2,1)S(1)}, u32[]{:S(2)}, u32[]{:S(2)}) collective-permute-start(bf16[320,1024]{1,0:T(8,128)(2,1)S(1)} %shard_map.44.refs_3_), channel_id=1, source_target_pairs={{0,32},{1,33},{2,34},{3,35},{8,10},{9,11},{10,8},{11,9},{16,48},{1... | collective-permute-start | bytes 1966088 | tf_op jit(solution)/shard_map/ppermute | solution.py:240
  60.9 1.5 %collective-permute-done.20.refs_1_ = f32[2,1024]{1,0:T(2,128)S(1)} collective-permute-done((f32[2,1024]{1,0:T(2,128)S(1)}, f32[2,1024]{1,0:T(2,128)S(1)}, u32[]{:S(2)}, u32[]{:S(2)}) %collective-permute-start.20) | collective-permute-done | bytes 8224 | tf_op jit(solution)/shard_map/ppermute | solution.py:228
  62.4 1.2 %collective-permute-done.22.refs_1_ = f32[2,1024]{1,0:T(2,128)S(1)} collective-permute-done((f32[2,1024]{1,0:T(2,128)S(1)}, f32[2,1024]{1,0:T(2,128)S(1)}, u32[]{:S(2)}, u32[]{:S(2)}) %collective-permute-start.22) | collective-permute-done | bytes 8224 | tf_op jit(solution)/shard_map/ppermute | solution.py:228
  63.5 1.7 %collective-permute-start.25 = (f32[2,1024]{1,0:T(2,128)S(1)}, f32[2,1024]{1,0:T(2,128)S(1)}, u32[]{:S(2)}, u32[]{:S(2)}) collective-permute-start(f32[2,1024]{1,0:T(2,128)S(1)} %shard_map.48.refs_0_), channel_id=1, source_target_pairs={{0,32},{1,33},{2,34},{3,35},{8,10},{9,11},{10,8},{11,9},{16,48},{1... | collective-permute-start | bytes 24584 | tf_op jit(solution)/shard_map/ppermute | solution.py:240
  65.3 2.1 %collective-permute-start.24 = (f32[2,1024]{1,0:T(2,128)S(1)}, f32[2,1024]{1,0:T(2,128)S(1)}, u32[]{:S(2)}, u32[]{:S(2)}) collective-permute-start(f32[2,1024]{1,0:T(2,128)S(1)} %shard_map.48.refs_0_), channel_id=1, source_target_pairs={{0,48},{1,49},{2,50},{3,51},{8,11},{9,8},{10,9},{11,10},{16,0},{17... | collective-permute-start | bytes 24584 | tf_op jit(solution)/shard_map/ppermute | solution.py:240
  67.4 1.0 %shard_map.41.own_ref = f32[320,1024]{1,0:T(8,128)S(1)} custom-call(bf16[320,1280]{1,0:T(8,128)(2,1)S(1)} %get-tuple-element.60.kernel_ref, bf16[560,1024]{1,0:T(8,128)(2,1)S(1)} %get-tuple-element.50.refs_1_.refs_0_, bf16[560,1024]{1,0:T(8,128)(2,1)S(1)} %get-tuple-element.51.refs_2_.refs_1_, bf16[80,1024]{1,0:T(8,128)(2,1)S(1)} %get-tuple-element.61.refs_2_, ...), custom_call_target="tpu_custom_call" | custom-call | tf_op jit(solution)/shard_map/pallas_call | solution.py:31
  68.5 4.8 %collective-permute-done.16.refs_4_.second_ref = bf16[320,1024]{1,0:T(8,128)(2,1)S(1)} collective-permute-done((bf16[320,1024]{1,0:T(8,128)(2,1)S(1)}, bf16[320,1024]{1,0:T(8,128)(2,1)S(1)}, u32[]{:S(2)}, u32[]{:S(2)}) %collective-permute-start.16) | collective-permute-done | bytes 655392 | tf_op jit(solution)/shard_map/ppermute | solution.py:240
  73.4 0.3 shard_map.50
  73.7 0.9 %collective-permute-start.26 = (bf16[96,1024]{1,0:T(8,128)(2,1)S(1)}, bf16[96,1024]{1,0:T(8,128)(2,1)S(1)}, u32[]{:S(2)}, u32[]{:S(2)}) collective-permute-start(bf16[96,1024]{1,0:T(8,128)(2,1)S(1)} %get-tuple-element.68), channel_id=1, source_target_pairs={{0,3},{1,0},{2,1},{3,2},{8,56},{9,57},{10,58},{11,59},{16,19},{17,... | collective-permute-start | bytes 589832 | tf_op jit(solution)/shard_map/ppermute | solution.py:240
  74.6 2.4 %collective-permute-start.27 = (bf16[96,1024]{1,0:T(8,128)(2,1)S(1)}, bf16[96,1024]{1,0:T(8,128)(2,1)S(1)}, u32[]{:S(2)}, u32[]{:S(2)}) collective-permute-start(bf16[96,1024]{1,0:T(8,128)(2,1)S(1)} %get-tuple-element.69), channel_id=1, source_target_pairs={{0,1},{1,2},{2,3},{3,0},{8,24},{9,25},{10,26},{11,27},{16,17},{17,... | collective-permute-start | bytes 589832 | tf_op jit(solution)/shard_map/ppermute | solution.py:240
  77.0 0.6 collective-permute-start.28
  77.6 3.1 %collective-permute-done.26.refs_0_ = bf16[96,1024]{1,0:T(8,128)(2,1)S(1)} collective-permute-done((bf16[96,1024]{1,0:T(8,128)(2,1)S(1)}, bf16[96,1024]{1,0:T(8,128)(2,1)S(1)}, u32[]{:S(2)}, u32[]{:S(2)}) %collective-permute-start.26) | collective-permute-done | bytes 196640 | tf_op jit(solution)/shard_map/ppermute | solution.py:240
  80.6 1.7 %collective-permute-done.27.refs_1_ = bf16[96,1024]{1,0:T(8,128)(2,1)S(1)} collective-permute-done((bf16[96,1024]{1,0:T(8,128)(2,1)S(1)}, bf16[96,1024]{1,0:T(8,128)(2,1)S(1)}, u32[]{:S(2)}, u32[]{:S(2)}) %collective-permute-start.27) | collective-permute-done | bytes 196640 | tf_op jit(solution)/shard_map/ppermute | solution.py:240
  82.3 1.8 %collective-permute-done.28.refs_2_ = bf16[96,1024]{1,0:T(8,128)(2,1)S(1)} collective-permute-done((bf16[96,1024]{1,0:T(8,128)(2,1)S(1)}, bf16[96,1024]{1,0:T(8,128)(2,1)S(1)}, u32[]{:S(2)}, u32[]{:S(2)}) %collective-permute-start.28) | collective-permute-done | bytes 196640 | tf_op jit(solution)/shard_map/ppermute | solution.py:240
  84.2 0.9 %shard_map.51 = f32[80,1024]{1,0:T(8,128)} custom-call(f32[80,1024]{1,0:T(8,128)S(1)} %get-tuple-element.67.own_ref, bf16[80,1152]{1,0:T(8,128)(2,1)S(1)} %shard_map.28.refs_0_.packed_ref, f32[2,1024]{1,0:T(2,128)S(1)} %shard_map.49.sums_ref, bf16[96,1024]{1,0:T(8,128)(2,1)S(1)} %collective-permute-done.26.refs_0_, ...), custom_call_target="tpu_custom_call" | custom-call | tf_op jit(solution)/shard_map/pallas_call | solution.py:31
  (38 shorter events, 0.4 us)
Async XLA Ops:
  0.0 0.9 %copy-start = (bf16[80,1024]{1,0:T(8,128)(2,1)S(1)}, bf16[80,1024]{1,0:T(8,128)(2,1)}, u32[]{:S(2)}) copy-start(bf16[80,1024]{1,0:T(8,128)(2,1)} %clips_hbm.1) | copy-start | bytes 491524
  0.9 0.7 copy-start.1
  2.1 10.6 %collective-permute-start.4 = (bf16[80,1152]{1,0:T(8,128)(2,1)S(1)}, bf16[80,1152]{1,0:T(8,128)(2,1)S(1)}, u32[]{:S(2)}, u32[]{:S(2)}) collective-permute-start(bf16[80,1152]{1,0:T(8,128)(2,1)S(1)} %shard_map.28.refs_0_.packed_ref), channel_id=1, source_target_pairs={{0,196},{4,0},{64,4},{68,64},{128,68},{132,128},{192,132},{196,192... | collective-permute-start | bytes 552968 | tf_op jit(solution)/shard_map/ppermute | solution.py:228
  8.0 7.9 %collective-permute-start.3 = (bf16[80,1152]{1,0:T(8,128)(2,1)S(1)}, bf16[80,1152]{1,0:T(8,128)(2,1)S(1)}, u32[]{:S(2)}, u32[]{:S(2)}) collective-permute-start(bf16[80,1152]{1,0:T(8,128)(2,1)S(1)} %shard_map.28.refs_0_.packed_ref), channel_id=1, source_target_pairs={{0,4},{4,64},{64,68},{68,128},{128,132},{132,192},{192,196},{196,0... | collective-permute-start | bytes 552968 | tf_op jit(solution)/shard_map/ppermute | solution.py:228
  8.0 7.9 %collective-permute-start.2 = (bf16[80,1152]{1,0:T(8,128)(2,1)S(1)}, bf16[80,1152]{1,0:T(8,128)(2,1)S(1)}, u32[]{:S(2)}, u32[]{:S(2)}) collective-permute-start(bf16[80,1152]{1,0:T(8,128)(2,1)S(1)} %shard_map.28.refs_0_.packed_ref), channel_id=1, source_target_pairs={{0,2},{1,3},{2,0},{3,1},{8,40},{9,41},{10,42},{11,43},{16,18},{17,... | collective-permute-start | bytes 552968 | tf_op jit(solution)/shard_map/ppermute | solution.py:240
  9.4 7.6 %collective-permute-start.1 = (bf16[80,1152]{1,0:T(8,128)(2,1)S(1)}, bf16[80,1152]{1,0:T(8,128)(2,1)S(1)}, u32[]{:S(2)}, u32[]{:S(2)}) collective-permute-start(bf16[80,1152]{1,0:T(8,128)(2,1)S(1)} %shard_map.28.refs_0_.packed_ref), channel_id=1, source_target_pairs={{0,3},{1,0},{2,1},{3,2},{8,56},{9,57},{10,58},{11,59},{16,19},{17,... | collective-permute-start | bytes 552968 | tf_op jit(solution)/shard_map/ppermute | solution.py:240
  9.4 7.6 %collective-permute-start = (bf16[80,1152]{1,0:T(8,128)(2,1)S(1)}, bf16[80,1152]{1,0:T(8,128)(2,1)S(1)}, u32[]{:S(2)}, u32[]{:S(2)}) collective-permute-start(bf16[80,1152]{1,0:T(8,128)(2,1)S(1)} %shard_map.28.refs_0_.packed_ref), channel_id=1, source_target_pairs={{0,1},{1,2},{2,3},{3,0},{8,24},{9,25},{10,26},{11,27},{16,17},{17,... | collective-permute-start | bytes 552968 | tf_op jit(solution)/shard_map/ppermute | solution.py:240
  12.6 9.7 %collective-permute-start.10 = (bf16[80,1152]{1,0:T(8,128)(2,1)S(1)}, bf16[80,1152]{1,0:T(8,128)(2,1)S(1)}, u32[]{:S(2)}, u32[]{:S(2)}) collective-permute-start(bf16[80,1152]{1,0:T(8,128)(2,1)S(1)} %collective-permute-done.4.refs_5_.refs_4_), channel_id=1, source_target_pairs={{0,196},{4,0},{64,4},{68,64},{128,68},{132,128},{192,132},{196,192... | collective-permute-start | bytes 552968 | tf_op jit(solution)/shard_map/ppermute | solution.py:228
  15.9 9.7 %collective-permute-start.8 = (bf16[80,1152]{1,0:T(8,128)(2,1)S(1)}, bf16[80,1152]{1,0:T(8,128)(2,1)S(1)}, u32[]{:S(2)}, u32[]{:S(2)}) collective-permute-start(bf16[80,1152]{1,0:T(8,128)(2,1)S(1)} %collective-permute-done.3.refs_4_.refs_1_), channel_id=1, source_target_pairs={{0,4},{4,64},{64,68},{68,128},{128,132},{132,192},{192,196},{196,0... | collective-permute-start | bytes 552968 | tf_op jit(solution)/shard_map/ppermute | solution.py:228
  17.1 16.0 %collective-permute-start.7 = (bf16[320,1152]{1,0:T(8,128)(2,1)S(1)}, bf16[320,1152]{1,0:T(8,128)(2,1)S(1)}, u32[]{:S(2)}, u32[]{:S(2)}) collective-permute-start(bf16[320,1152]{1,0:T(8,128)(2,1)S(1)} %shard_map.29.refs_3_), channel_id=1, source_target_pairs={{0,32},{1,33},{2,34},{3,35},{8,10},{9,11},{10,8},{11,9},{16,48},{1... | collective-permute-start | bytes 2211848 | tf_op jit(solution)/shard_map/ppermute | solution.py:240
  20.4 18.1 %collective-permute-start.6 = (bf16[320,1152]{1,0:T(8,128)(2,1)S(1)}, bf16[320,1152]{1,0:T(8,128)(2,1)S(1)}, u32[]{:S(2)}, u32[]{:S(2)}) collective-permute-start(bf16[320,1152]{1,0:T(8,128)(2,1)S(1)} %shard_map.29.refs_3_), channel_id=1, source_target_pairs={{0,48},{1,49},{2,50},{3,51},{8,11},{9,8},{10,9},{11,10},{16,0},{17... | collective-permute-start | bytes 2211848 | tf_op jit(solution)/shard_map/ppermute | solution.py:240
  21.4 17.0 %collective-permute-start.5 = (bf16[320,1152]{1,0:T(8,128)(2,1)S(1)}, bf16[320,1152]{1,0:T(8,128)(2,1)S(1)}, u32[]{:S(2)}, u32[]{:S(2)}) collective-permute-start(bf16[320,1152]{1,0:T(8,128)(2,1)S(1)} %shard_map.29.refs_3_), channel_id=1, source_target_pairs={{0,16},{1,17},{2,18},{3,19},{8,9},{9,10},{10,11},{11,8},{16,32},{1... | collective-permute-start | bytes 2211848 | tf_op jit(solution)/shard_map/ppermute | solution.py:240
  22.4 6.3 %collective-permute-start.11 = (bf16[80,1152]{1,0:T(8,128)(2,1)S(1)}, bf16[80,1152]{1,0:T(8,128)(2,1)S(1)}, u32[]{:S(2)}, u32[]{:S(2)}) collective-permute-start(bf16[80,1152]{1,0:T(8,128)(2,1)S(1)} %collective-permute-done.10.refs_5_), channel_id=1, source_target_pairs={{0,196},{4,0},{64,4},{68,64},{128,68},{132,128},{192,132},{196,192... | collective-permute-start | bytes 552968 | tf_op jit(solution)/shard_map/ppermute | solution.py:228
  25.6 6.7 %collective-permute-start.9 = (bf16[80,1152]{1,0:T(8,128)(2,1)S(1)}, bf16[80,1152]{1,0:T(8,128)(2,1)S(1)}, u32[]{:S(2)}, u32[]{:S(2)}) collective-permute-start(bf16[80,1152]{1,0:T(8,128)(2,1)S(1)} %collective-permute-done.8.refs_2_), channel_id=1, source_target_pairs={{0,4},{4,64},{64,68},{68,128},{128,132},{132,192},{192,196},{196,0... | collective-permute-start | bytes 552968 | tf_op jit(solution)/shard_map/ppermute | solution.py:228
  32.5 6.0 %collective-permute-start.12 = (bf16[560,1152]{1,0:T(8,128)(2,1)S(1)}, bf16[560,1152]{1,0:T(8,128)(2,1)S(1)}, u32[]{:S(2)}, u32[]{:S(2)}) collective-permute-start(bf16[560,1152]{1,0:T(8,128)(2,1)S(1)} %shard_map.34.block_ref.refs_4_), channel_id=1, source_target_pairs={{0,8},{8,0},{1,9},{9,1},{2,10},{10,2},{3,11},{11,3},{4,12},{12,4},... | collective-permute-start | bytes 3870728 | tf_op jit(solution)/shard_map/ppermute | solution.py:228
  33.0 7.1 %collective-permute-start.13 = (bf16[80,1152]{1,0:T(8,128)(2,1)S(1)}, bf16[80,1152]{1,0:T(8,128)(2,1)S(1)}, u32[]{:S(2)}, u32[]{:S(2)}) collective-permute-start(bf16[80,1152]{1,0:T(8,128)(2,1)S(1)} %collective-permute-done.11.refs_6_), channel_id=1, source_target_pairs={{0,196},{4,0},{64,4},{68,64},{128,68},{132,128},{192,132},{196,192... | collective-permute-start | bytes 552968 | tf_op jit(solution)/shard_map/ppermute | solution.py:228
  40.1 1.7 %collective-permute-start.14 = (bf16[80,1152]{1,0:T(8,128)(2,1)S(1)}, bf16[80,1152]{1,0:T(8,128)(2,1)S(1)}, u32[]{:S(2)}, u32[]{:S(2)}) collective-permute-start(bf16[80,1152]{1,0:T(8,128)(2,1)S(1)} %shard_map.37.block_ref.refs_6_), channel_id=1, source_target_pairs={{0,8},{8,0},{1,9},{9,1},{2,10},{10,2},{3,11},{11,3},{4,12},{12,4},... | collective-permute-start | bytes 552968 | tf_op jit(solution)/shard_map/ppermute | solution.py:228
  47.7 15.9 %collective-permute-start.15 = (bf16[320,1024]{1,0:T(8,128)(2,1)S(1)}, bf16[320,1024]{1,0:T(8,128)(2,1)S(1)}, u32[]{:S(2)}, u32[]{:S(2)}) collective-permute-start(bf16[320,1024]{1,0:T(8,128)(2,1)S(1)} %shard_map.42.refs_3_), channel_id=1, source_target_pairs={{0,48},{1,49},{2,50},{3,51},{8,11},{9,8},{10,9},{11,10},{16,0},{17... | collective-permute-start | bytes 1966088 | tf_op jit(solution)/shard_map/ppermute | solution.py:240
  50.0 4.9 %collective-permute-start.18 = (f32[2,1024]{1,0:T(2,128)S(1)}, f32[2,1024]{1,0:T(2,128)S(1)}, u32[]{:S(2)}, u32[]{:S(2)}) collective-permute-start(f32[2,1024]{1,0:T(2,128)S(1)} %get-tuple-element.66.refs_0_), channel_id=1, source_target_pairs={{0,4},{4,64},{64,68},{68,128},{128,132},{132,192},{192,196},{196,0... | collective-permute-start | bytes 24584 | tf_op jit(solution)/shard_map/ppermute | solution.py:228
  50.0 5.7 %collective-permute-start.19 = (f32[2,1024]{1,0:T(2,128)S(1)}, f32[2,1024]{1,0:T(2,128)S(1)}, u32[]{:S(2)}, u32[]{:S(2)}) collective-permute-start(f32[2,1024]{1,0:T(2,128)S(1)} %get-tuple-element.66.refs_0_), channel_id=1, source_target_pairs={{0,196},{4,0},{64,4},{68,64},{128,68},{132,128},{192,132},{196,192... | collective-permute-start | bytes 24584 | tf_op jit(solution)/shard_map/ppermute | solution.py:228
  54.3 19.0 %collective-permute-start.16 = (bf16[320,1024]{1,0:T(8,128)(2,1)S(1)}, bf16[320,1024]{1,0:T(8,128)(2,1)S(1)}, u32[]{:S(2)}, u32[]{:S(2)}) collective-permute-start(bf16[320,1024]{1,0:T(8,128)(2,1)S(1)} %shard_map.43.refs_4_), channel_id=1, source_target_pairs={{0,16},{1,17},{2,18},{3,19},{8,9},{9,10},{10,11},{11,8},{16,32},{1... | collective-permute-start | bytes 1966088 | tf_op jit(solution)/shard_map/ppermute | solution.py:240
  54.9 6.0 %collective-permute-start.21 = (f32[2,1024]{1,0:T(2,128)S(1)}, f32[2,1024]{1,0:T(2,128)S(1)}, u32[]{:S(2)}, u32[]{:S(2)}) collective-permute-start(f32[2,1024]{1,0:T(2,128)S(1)} %shard_map.46), channel_id=1, source_target_pairs={{0,132},{4,192},{64,196},{68,0},{128,4},{132,64},{192,68},{196,128... | collective-permute-start | bytes 24584 | tf_op jit(solution)/shard_map/ppermute | solution.py:228
  55.7 6.7 %collective-permute-start.20 = (f32[2,1024]{1,0:T(2,128)S(1)}, f32[2,1024]{1,0:T(2,128)S(1)}, u32[]{:S(2)}, u32[]{:S(2)}) collective-permute-start(f32[2,1024]{1,0:T(2,128)S(1)} %shard_map.45.refs_0_), channel_id=1, source_target_pairs={{0,68},{4,128},{64,132},{68,192},{128,196},{132,0},{192,4},{196,64... | collective-permute-start | bytes 24584 | tf_op jit(solution)/shard_map/ppermute | solution.py:228
  59.8 13.6 %collective-permute-start.17 = (bf16[320,1024]{1,0:T(8,128)(2,1)S(1)}, bf16[320,1024]{1,0:T(8,128)(2,1)S(1)}, u32[]{:S(2)}, u32[]{:S(2)}) collective-permute-start(bf16[320,1024]{1,0:T(8,128)(2,1)S(1)} %shard_map.44.refs_3_), channel_id=1, source_target_pairs={{0,32},{1,33},{2,34},{3,35},{8,10},{9,11},{10,8},{11,9},{16,48},{1... | collective-permute-start | bytes 1966088 | tf_op jit(solution)/shard_map/ppermute | solution.py:240
  62.4 1.2 %collective-permute-start.22 = (f32[2,1024]{1,0:T(2,128)S(1)}, f32[2,1024]{1,0:T(2,128)S(1)}, u32[]{:S(2)}, u32[]{:S(2)}) collective-permute-start(f32[2,1024]{1,0:T(2,128)S(1)} %shard_map.47.refs_0_), channel_id=1, source_target_pairs={{0,8},{8,0},{1,9},{9,1},{2,10},{10,2},{3,11},{11,3},{4,12},{12,4},... | collective-permute-start | bytes 24584 | tf_op jit(solution)/shard_map/ppermute | solution.py:228
  63.5 9.7 %collective-permute-start.25 = (f32[2,1024]{1,0:T(2,128)S(1)}, f32[2,1024]{1,0:T(2,128)S(1)}, u32[]{:S(2)}, u32[]{:S(2)}) collective-permute-start(f32[2,1024]{1,0:T(2,128)S(1)} %shard_map.48.refs_0_), channel_id=1, source_target_pairs={{0,32},{1,33},{2,34},{3,35},{8,10},{9,11},{10,8},{11,9},{16,48},{1... | collective-permute-start | bytes 24584 | tf_op jit(solution)/shard_map/ppermute | solution.py:240
  65.3 8.0 %collective-permute-start.24 = (f32[2,1024]{1,0:T(2,128)S(1)}, f32[2,1024]{1,0:T(2,128)S(1)}, u32[]{:S(2)}, u32[]{:S(2)}) collective-permute-start(f32[2,1024]{1,0:T(2,128)S(1)} %shard_map.48.refs_0_), channel_id=1, source_target_pairs={{0,48},{1,49},{2,50},{3,51},{8,11},{9,8},{10,9},{11,10},{16,0},{17... | collective-permute-start | bytes 24584 | tf_op jit(solution)/shard_map/ppermute | solution.py:240
  67.4 6.0 %collective-permute-start.23 = (f32[2,1024]{1,0:T(2,128)S(1)}, f32[2,1024]{1,0:T(2,128)S(1)}, u32[]{:S(2)}, u32[]{:S(2)}) collective-permute-start(f32[2,1024]{1,0:T(2,128)S(1)} %shard_map.48.refs_0_), channel_id=1, source_target_pairs={{0,16},{1,17},{2,18},{3,19},{8,9},{9,10},{10,11},{11,8},{16,32},{1... | collective-permute-start | bytes 24584 | tf_op jit(solution)/shard_map/ppermute | solution.py:240
  73.7 7.0 %collective-permute-start.26 = (bf16[96,1024]{1,0:T(8,128)(2,1)S(1)}, bf16[96,1024]{1,0:T(8,128)(2,1)S(1)}, u32[]{:S(2)}, u32[]{:S(2)}) collective-permute-start(bf16[96,1024]{1,0:T(8,128)(2,1)S(1)} %get-tuple-element.68), channel_id=1, source_target_pairs={{0,3},{1,0},{2,1},{3,2},{8,56},{9,57},{10,58},{11,59},{16,19},{17,... | collective-permute-start | bytes 589832 | tf_op jit(solution)/shard_map/ppermute | solution.py:240
  74.6 7.7 %collective-permute-start.27 = (bf16[96,1024]{1,0:T(8,128)(2,1)S(1)}, bf16[96,1024]{1,0:T(8,128)(2,1)S(1)}, u32[]{:S(2)}, u32[]{:S(2)}) collective-permute-start(bf16[96,1024]{1,0:T(8,128)(2,1)S(1)} %get-tuple-element.69), channel_id=1, source_target_pairs={{0,1},{1,2},{2,3},{3,0},{8,24},{9,25},{10,26},{11,27},{16,17},{17,... | collective-permute-start | bytes 589832 | tf_op jit(solution)/shard_map/ppermute | solution.py:240
  77.0 7.2 %collective-permute-start.28 = (bf16[96,1024]{1,0:T(8,128)(2,1)S(1)}, bf16[96,1024]{1,0:T(8,128)(2,1)S(1)}, u32[]{:S(2)}, u32[]{:S(2)}) collective-permute-start(bf16[96,1024]{1,0:T(8,128)(2,1)S(1)} %get-tuple-element.70), channel_id=1, source_target_pairs={{0,2},{1,3},{2,0},{3,1},{8,40},{9,41},{10,42},{11,43},{16,18},{17,... | collective-permute-start | bytes 589832 | tf_op jit(solution)/shard_map/ppermute | solution.py:240

commit v3 on v2

--- a/solution.py
+++ b/solution.py
@@ -239,6 +239,14 @@
                     pairs.append(((y * 2 + core) * 4 + x, (to_y * 2 + core) * 4 + to_x))
         return lax.ppermute(value, PLANE, pairs)
 
+    def cross_shift(value):
+        pairs = []
+        for core in range(2):
+            for z in range(8):
+                to_z, to_core = (z + 1) % 8, 1 - core
+                pairs.append((z // 2 * 4 + core * 2 + z % 2, to_z // 2 * 4 + to_core * 2 + to_z % 2))
+        return lax.ppermute(value, ("z_hi", "core", "z_lo"), pairs)
+
     own = pl.pallas_call(
         pack_kernel,
         out_shape=shape((ROWS, WIDE), BF16),
@@ -264,14 +272,14 @@
     down.append(shift(down[2], Z, -1))
     up.append(shift(down[3], Z, -1))
 
+    cross = cross_shift(up[3])
     blocks = [join([own, *up[1:4], *down[1:4]])]
     blocks += [shift(block, "core", 1) for block in blocks]
     early = [prep(block) for block in blocks]
-    blocks.append(join([up[4]], after=[member for member, _, _ in early], flops=0))
-    blocks.append(shift(blocks[-1], "core", 1))
+    blocks += [up[4], cross]
     members, lines, counts = zip(*early, *[prep(block) for block in blocks[2:]])
 
-    for _ in range(4):
+    for _ in range(3):
         rows = relay(rows, flops=3 * 10**9)
     *kernel, sums = kernels([*rows, four], blocks, lines, counts)
     terms = [main(part, BF16, members) for part in kernel[:3]]

time: 85.2 us -> 91.5 us (1.074)
  waiting for transfers between devices: 30.3 us -> 35.8 us
    ppermute x0 -> x1, waiting for transfers between devices: none -> 7.35 us  [cross_shift(): return lax.ppermute(value, ('z_hi', 'core', 'z_lo'), pairs)]
    ppermute x15, waiting for transfers between devices: 17.9 us -> 12.4 us  [plane_shift(): return lax.ppermute(value, PLANE, pairs)]
    ppermute x14 -> x13, waiting for transfers between devices: 12.3 us -> 16.1 us  [shift(): return lax.ppermute(value, axis, pairs)]
    ppermute x15, starting transfers between devices: 21.3 us -> 22.3 us  [plane_shift(): return lax.ppermute(value, PLANE, pairs)]
    ppermute x14 -> x13, starting transfers between devices: 19.9 us -> 19.6 us  [shift(): return lax.ppermute(value, axis, pairs)]
    pallas_call x19 -> x18, Pallas kernels: 11.4 us -> 11.4 us  [call(): pl.pallas_call(body, out_shape=outs, compiler_params=pltpu.CompilerParams...]
  transfers between devices with their start and end apart: 29 -> 29, of which waited for: 14 -> 13; matrix products, arithmetic and copies ran while one was open for 0% -> 0% of each run, Pallas kernels for 5% -> 4%
where the time goes in v3:
time: 91.5 us; the launch traced here: 91.4 us
  starting transfers between devices  41.9 us (46%)
  waiting for transfers between devices  35.8 us (39%)
  Pallas kernels  11.8 us (13%)
  local copies, waits for them, and re-layouts  1.57 us (2%)
    ppermute x15, starting transfers between devices, plane_shift(): return lax.ppermute(value, PLANE, pairs)  22.3 us
    ppermute x13, starting transfers between devices, shift(): return lax.ppermute(value, axis, pairs)  19.6 us
    ppermute x13, waiting for transfers between devices, shift(): return lax.ppermute(value, axis, pairs)  16.1 us
    ppermute x15, waiting for transfers between devices, plane_shift(): return lax.ppermute(value, PLANE, pairs)  12.4 us
    pallas_call x18, Pallas kernels, call(): pl.pallas_call(body, out_shape=outs, compiler_params=pltpu.CompilerParams...  11.4 us
    ppermute x1, waiting for transfers between devices, cross_shift(): return lax.ppermute(value, ('z_hi', 'core', 'z_lo'), pairs)  7.35 us
  transfers between devices with their start and end apart: 29, of which 13 were waited for; matrix products, arithmetic and copies ran while one was open for 0% of the time, Pallas kernels for 4%

profile of v3, /device:TPU:6, one launch (start us, length us, event | category | flops | bytes accessed | tf_op | source)
XLA Modules:
  0.0 91.4 jit_solution(2114522548715987561)
XLA Ops:
  0.0 0.9 copy-done
  0.9 0.7 copy-done.1
  1.6 0.5 shard_map.28.refs_0_.packed_ref
  2.1 5.9 %collective-permute-start.4 = (bf16[80,1152]{1,0:T(8,128)(2,1)S(1)}, bf16[80,1152]{1,0:T(8,128)(2,1)S(1)}, u32[]{:S(2)}, u32[]{:S(2)}) collective-permute-start(bf16[80,1152]{1,0:T(8,128)(2,1)S(1)} %shard_map.28.refs_0_.packed_ref), channel_id=1, source_target_pairs={{0,196},{4,0},{64,4},{68,64},{128,68},{132,128},{192,132},{196,192... | collective-permute-start | bytes 552968 | tf_op jit(solution)/shard_map/ppermute | solution.py:228
  8.0 1.4 %collective-permute-start.2 = (bf16[80,1152]{1,0:T(8,128)(2,1)S(1)}, bf16[80,1152]{1,0:T(8,128)(2,1)S(1)}, u32[]{:S(2)}, u32[]{:S(2)}) collective-permute-start(bf16[80,1152]{1,0:T(8,128)(2,1)S(1)} %shard_map.28.refs_0_.packed_ref), channel_id=1, source_target_pairs={{0,2},{1,3},{2,0},{3,1},{8,40},{9,41},{10,42},{11,43},{16,18},{17,... | collective-permute-start | bytes 552968 | tf_op jit(solution)/shard_map/ppermute | solution.py:240
  9.4 3.2 %collective-permute-start = (bf16[80,1152]{1,0:T(8,128)(2,1)S(1)}, bf16[80,1152]{1,0:T(8,128)(2,1)S(1)}, u32[]{:S(2)}, u32[]{:S(2)}) collective-permute-start(bf16[80,1152]{1,0:T(8,128)(2,1)S(1)} %shard_map.28.refs_0_.packed_ref), channel_id=1, source_target_pairs={{0,1},{1,2},{2,3},{3,0},{8,24},{9,25},{10,26},{11,27},{16,17},{17,... | collective-permute-start | bytes 552968 | tf_op jit(solution)/shard_map/ppermute | solution.py:240
  12.6 3.2 %collective-permute-start.10 = (bf16[80,1152]{1,0:T(8,128)(2,1)S(1)}, bf16[80,1152]{1,0:T(8,128)(2,1)S(1)}, u32[]{:S(2)}, u32[]{:S(2)}) collective-permute-start(bf16[80,1152]{1,0:T(8,128)(2,1)S(1)} %collective-permute-done.4.refs_5_.refs_4_), channel_id=1, source_target_pairs={{0,196},{4,0},{64,4},{68,64},{128,68},{132,128},{192,132},{196,192... | collective-permute-start | bytes 552968 | tf_op jit(solution)/shard_map/ppermute | solution.py:228
  15.9 1.1 %collective-permute-done.1.refs_2_ = bf16[80,1152]{1,0:T(8,128)(2,1)S(1)} collective-permute-done((bf16[80,1152]{1,0:T(8,128)(2,1)S(1)}, bf16[80,1152]{1,0:T(8,128)(2,1)S(1)}, u32[]{:S(2)}, u32[]{:S(2)}) %collective-permute-start.1) | collective-permute-done | bytes 184352 | tf_op jit(solution)/shard_map/ppermute | solution.py:240
  17.1 3.3 %collective-permute-start.7 = (bf16[320,1152]{1,0:T(8,128)(2,1)S(1)}, bf16[320,1152]{1,0:T(8,128)(2,1)S(1)}, u32[]{:S(2)}, u32[]{:S(2)}) collective-permute-start(bf16[320,1152]{1,0:T(8,128)(2,1)S(1)} %shard_map.29.refs_3_), channel_id=1, source_target_pairs={{0,32},{1,33},{2,34},{3,35},{8,10},{9,11},{10,8},{11,9},{16,48},{1... | collective-permute-start | bytes 2211848 | tf_op jit(solution)/shard_map/ppermute | solution.py:240
  20.4 1.1 %collective-permute-start.6 = (bf16[320,1152]{1,0:T(8,128)(2,1)S(1)}, bf16[320,1152]{1,0:T(8,128)(2,1)S(1)}, u32[]{:S(2)}, u32[]{:S(2)}) collective-permute-start(bf16[320,1152]{1,0:T(8,128)(2,1)S(1)} %shard_map.29.refs_3_), channel_id=1, source_target_pairs={{0,48},{1,49},{2,50},{3,51},{8,11},{9,8},{10,9},{11,10},{16,0},{17... | collective-permute-start | bytes 2211848 | tf_op jit(solution)/shard_map/ppermute | solution.py:240
  21.4 1.0 %collective-permute-start.5 = (bf16[320,1152]{1,0:T(8,128)(2,1)S(1)}, bf16[320,1152]{1,0:T(8,128)(2,1)S(1)}, u32[]{:S(2)}, u32[]{:S(2)}) collective-permute-start(bf16[320,1152]{1,0:T(8,128)(2,1)S(1)} %shard_map.29.refs_3_), channel_id=1, source_target_pairs={{0,16},{1,17},{2,18},{3,19},{8,9},{9,10},{10,11},{11,8},{16,32},{1... | collective-permute-start | bytes 2211848 | tf_op jit(solution)/shard_map/ppermute | solution.py:240
  22.4 3.2 %collective-permute-start.11 = (bf16[80,1152]{1,0:T(8,128)(2,1)S(1)}, bf16[80,1152]{1,0:T(8,128)(2,1)S(1)}, u32[]{:S(2)}, u32[]{:S(2)}) collective-permute-start(bf16[80,1152]{1,0:T(8,128)(2,1)S(1)} %collective-permute-done.10.refs_5_), channel_id=1, source_target_pairs={{0,196},{4,0},{64,4},{68,64},{128,68},{132,128},{192,132},{196,192... | collective-permute-start | bytes 552968 | tf_op jit(solution)/shard_map/ppermute | solution.py:228
  25.6 3.1 %collective-permute-done.11.refs_6_ = bf16[80,1152]{1,0:T(8,128)(2,1)S(1)} collective-permute-done((bf16[80,1152]{1,0:T(8,128)(2,1)S(1)}, bf16[80,1152]{1,0:T(8,128)(2,1)S(1)}, u32[]{:S(2)}, u32[]{:S(2)}) %collective-permute-start.11) | collective-permute-done | bytes 184352 | tf_op jit(solution)/shard_map/ppermute | solution.py:228
  28.7 3.7 %collective-permute-done.9.refs_3_ = bf16[80,1152]{1,0:T(8,128)(2,1)S(1)} collective-permute-done((bf16[80,1152]{1,0:T(8,128)(2,1)S(1)}, bf16[80,1152]{1,0:T(8,128)(2,1)S(1)}, u32[]{:S(2)}, u32[]{:S(2)}) %collective-permute-start.9) | collective-permute-done | bytes 184352 | tf_op jit(solution)/shard_map/ppermute | solution.py:228
  32.4 0.1 shard_map.33.block_ref.refs_4_
  32.5 0.1 collective-permute-start.12
  32.6 0.1 collective-permute-start.13
  32.7 7.0 %collective-permute-done.13.block_ref.refs_6_ = bf16[80,1152]{1,0:T(8,128)(2,1)S(1)} collective-permute-done((bf16[80,1152]{1,0:T(8,128)(2,1)S(1)}, bf16[80,1152]{1,0:T(8,128)(2,1)S(1)}, u32[]{:S(2)}, u32[]{:S(2)}) %collective-permute-start.13) | collective-permute-done | bytes 184352 | tf_op jit(solution)/shard_map/ppermute | solution.py:228
  39.6 0.4 shard_map.34
  40.1 0.2 shard_map.36
  40.2 7.4 %collective-permute-done.14.block_ref.refs_7_ = bf16[80,1152]{1,0:T(8,128)(2,1)S(1)} collective-permute-done((bf16[80,1152]{1,0:T(8,128)(2,1)S(1)}, bf16[80,1152]{1,0:T(8,128)(2,1)S(1)}, u32[]{:S(2)}, u32[]{:S(2)}) %collective-permute-start.14) | collective-permute-done | bytes 184352 | tf_op jit(solution)/shard_map/ppermute | solution.py:248
  47.6 0.2 shard_map.37
  47.9 0.4 shard_map.35
  48.3 4.6 %shard_map.38 = (bf16[320,1280]{1,0:T(8,128)(2,1)S(1)}, bf16[320,1280]{1,0:T(8,128)(2,1)S(1)}, bf16[320,1280]{1,0:T(8,128)(2,1)S(1)}, bf16[320,1280]{1,0:T(8,128)(2,1)S(1)}, f32[2,1024]{1,0:T(2,128)S(1)}) custom-call(bf16[320,1152]{1,0:T(8,128)(2,1)S(1)} %get-tuple-element.41.refs_0_, bf16[320,1152]{1,0:T(8,128)(2,1)S(1)} %get-tuple-element.42.refs_1_, ...), custom_call_target="tpu_custom_call" | custom-call | tf_op jit(solution)/shard_map/pallas_call | solution.py:31
  52.9 1.0 %shard_map.40.refs_3_ = bf16[320,1024]{1,0:T(8,128)(2,1)S(1)} custom-call(bf16[320,1280]{1,0:T(8,128)(2,1)S(1)} %get-tuple-element.57.kernel_ref, bf16[560,1024]{1,0:T(8,128)(2,1)S(1)} %get-tuple-element.53.refs_0_, bf16[560,1024]{1,0:T(8,128)(2,1)S(1)} %get-tuple-element.54.refs_1_, bf16[80,1024]{1,0:T(8,128)(2,1)S(1)} %get-tuple-element.55.refs_2_, ...), custom_call_target="tpu_custom_call" | custom-call | tf_op jit(solution)/shard_map/pallas_call | solution.py:31
  53.9 2.3 %collective-permute-start.15 = (bf16[320,1024]{1,0:T(8,128)(2,1)S(1)}, bf16[320,1024]{1,0:T(8,128)(2,1)S(1)}, u32[]{:S(2)}, u32[]{:S(2)}) collective-permute-start(bf16[320,1024]{1,0:T(8,128)(2,1)S(1)} %shard_map.40.refs_3_), channel_id=1, source_target_pairs={{0,48},{1,49},{2,50},{3,51},{8,11},{9,8},{10,9},{11,10},{16,0},{17... | collective-permute-start | bytes 1966088 | tf_op jit(solution)/shard_map/ppermute | solution.py:240
  56.3 3.2 %collective-permute-start.19 = (f32[2,1024]{1,0:T(2,128)S(1)}, f32[2,1024]{1,0:T(2,128)S(1)}, u32[]{:S(2)}, u32[]{:S(2)}) collective-permute-start(f32[2,1024]{1,0:T(2,128)S(1)} %get-tuple-element.60.refs_0_), channel_id=1, source_target_pairs={{0,196},{4,0},{64,4},{68,64},{128,68},{132,128},{192,132},{196,192... | collective-permute-start | bytes 24584 | tf_op jit(solution)/shard_map/ppermute | solution.py:228
  59.5 1.0 %shard_map.41.refs_4_ = bf16[320,1024]{1,0:T(8,128)(2,1)S(1)} custom-call(bf16[320,1280]{1,0:T(8,128)(2,1)S(1)} %get-tuple-element.58.kernel_ref, bf16[560,1024]{1,0:T(8,128)(2,1)S(1)} %get-tuple-element.53.refs_0_, bf16[560,1024]{1,0:T(8,128)(2,1)S(1)} %get-tuple-element.54.refs_1_, bf16[80,1024]{1,0:T(8,128)(2,1)S(1)} %get-tuple-element.55.refs_2_, ...), custom_call_target="tpu_custom_call" | custom-call | tf_op jit(solution)/shard_map/pallas_call | solution.py:31
  60.6 0.1 collective-permute-start.16
  60.6 0.5 collective-permute-done.18.refs_1_
  61.2 3.8 %collective-permute-start.20 = (f32[2,1024]{1,0:T(2,128)S(1)}, f32[2,1024]{1,0:T(2,128)S(1)}, u32[]{:S(2)}, u32[]{:S(2)}) collective-permute-start(f32[2,1024]{1,0:T(2,128)S(1)} %shard_map.43.refs_0_), channel_id=1, source_target_pairs={{0,68},{4,128},{64,132},{68,192},{128,196},{132,0},{192,4},{196,64... | collective-permute-start | bytes 24584 | tf_op jit(solution)/shard_map/ppermute | solution.py:228
  65.0 1.0 %shard_map.42.refs_3_ = bf16[320,1024]{1,0:T(8,128)(2,1)S(1)} custom-call(bf16[320,1280]{1,0:T(8,128)(2,1)S(1)} %get-tuple-element.59.kernel_ref, bf16[560,1024]{1,0:T(8,128)(2,1)S(1)} %get-tuple-element.53.refs_0_, bf16[560,1024]{1,0:T(8,128)(2,1)S(1)} %get-tuple-element.54.refs_1_, bf16[80,1024]{1,0:T(8,128)(2,1)S(1)} %get-tuple-element.55.refs_2_, ...), custom_call_target="tpu_custom_call" | custom-call | tf_op jit(solution)/shard_map/pallas_call | solution.py:31
  66.0 1.2 %collective-permute-start.17 = (bf16[320,1024]{1,0:T(8,128)(2,1)S(1)}, bf16[320,1024]{1,0:T(8,128)(2,1)S(1)}, u32[]{:S(2)}, u32[]{:S(2)}) collective-permute-start(bf16[320,1024]{1,0:T(8,128)(2,1)S(1)} %shard_map.42.refs_3_), channel_id=1, source_target_pairs={{0,32},{1,33},{2,34},{3,35},{8,10},{9,11},{10,8},{11,9},{16,48},{1... | collective-permute-start | bytes 1966088 | tf_op jit(solution)/shard_map/ppermute | solution.py:240
  67.2 0.7 collective-permute-done.20.refs_1_
  67.9 1.2 %collective-permute-done.22.refs_1_ = f32[2,1024]{1,0:T(2,128)S(1)} collective-permute-done((f32[2,1024]{1,0:T(2,128)S(1)}, f32[2,1024]{1,0:T(2,128)S(1)}, u32[]{:S(2)}, u32[]{:S(2)}) %collective-permute-start.22) | collective-permute-done | bytes 8224 | tf_op jit(solution)/shard_map/ppermute | solution.py:228
  69.1 2.1 %collective-permute-start.25 = (f32[2,1024]{1,0:T(2,128)S(1)}, f32[2,1024]{1,0:T(2,128)S(1)}, u32[]{:S(2)}, u32[]{:S(2)}) collective-permute-start(f32[2,1024]{1,0:T(2,128)S(1)} %shard_map.46.refs_0_), channel_id=1, source_target_pairs={{0,32},{1,33},{2,34},{3,35},{8,10},{9,11},{10,8},{11,9},{16,48},{1... | collective-permute-start | bytes 24584 | tf_op jit(solution)/shard_map/ppermute | solution.py:240
  71.1 2.7 %collective-permute-start.24 = (f32[2,1024]{1,0:T(2,128)S(1)}, f32[2,1024]{1,0:T(2,128)S(1)}, u32[]{:S(2)}, u32[]{:S(2)}) collective-permute-start(f32[2,1024]{1,0:T(2,128)S(1)} %shard_map.46.refs_0_), channel_id=1, source_target_pairs={{0,48},{1,49},{2,50},{3,51},{8,11},{9,8},{10,9},{11,10},{16,0},{17... | collective-permute-start | bytes 24584 | tf_op jit(solution)/shard_map/ppermute | solution.py:240
  73.9 1.0 %shard_map.39.own_ref = f32[320,1024]{1,0:T(8,128)S(1)} custom-call(bf16[320,1280]{1,0:T(8,128)(2,1)S(1)} %get-tuple-element.52.kernel_ref, bf16[560,1024]{1,0:T(8,128)(2,1)S(1)} %get-tuple-element.53.refs_0_, bf16[560,1024]{1,0:T(8,128)(2,1)S(1)} %get-tuple-element.54.refs_1_, bf16[80,1024]{1,0:T(8,128)(2,1)S(1)} %get-tuple-element.55.refs_2_, ...), custom_call_target="tpu_custom_call" | custom-call | tf_op jit(solution)/shard_map/pallas_call | solution.py:31
  74.9 4.6 %collective-permute-done.16.refs_4_.second_ref = bf16[320,1024]{1,0:T(8,128)(2,1)S(1)} collective-permute-done((bf16[320,1024]{1,0:T(8,128)(2,1)S(1)}, bf16[320,1024]{1,0:T(8,128)(2,1)S(1)}, u32[]{:S(2)}, u32[]{:S(2)}) %collective-permute-start.16) | collective-permute-done | bytes 655392 | tf_op jit(solution)/shard_map/ppermute | solution.py:240
  79.5 0.1 collective-permute-done.23.refs_1_
  79.6 0.3 shard_map.48
  79.9 0.9 collective-permute-start.26
  80.8 2.4 %collective-permute-start.27 = (bf16[96,1024]{1,0:T(8,128)(2,1)S(1)}, bf16[96,1024]{1,0:T(8,128)(2,1)S(1)}, u32[]{:S(2)}, u32[]{:S(2)}) collective-permute-start(bf16[96,1024]{1,0:T(8,128)(2,1)S(1)} %get-tuple-element.63), channel_id=1, source_target_pairs={{0,1},{1,2},{2,3},{3,0},{8,24},{9,25},{10,26},{11,27},{16,17},{17,... | collective-permute-start | bytes 589832 | tf_op jit(solution)/shard_map/ppermute | solution.py:240
  83.3 0.6 collective-permute-start.28
  83.9 3.0 %collective-permute-done.26.refs_0_ = bf16[96,1024]{1,0:T(8,128)(2,1)S(1)} collective-permute-done((bf16[96,1024]{1,0:T(8,128)(2,1)S(1)}, bf16[96,1024]{1,0:T(8,128)(2,1)S(1)}, u32[]{:S(2)}, u32[]{:S(2)}) %collective-permute-start.26) | collective-permute-done | bytes 196640 | tf_op jit(solution)/shard_map/ppermute | solution.py:240
  86.9 1.7 %collective-permute-done.27.refs_1_ = bf16[96,1024]{1,0:T(8,128)(2,1)S(1)} collective-permute-done((bf16[96,1024]{1,0:T(8,128)(2,1)S(1)}, bf16[96,1024]{1,0:T(8,128)(2,1)S(1)}, u32[]{:S(2)}, u32[]{:S(2)}) %collective-permute-start.27) | collective-permute-done | bytes 196640 | tf_op jit(solution)/shard_map/ppermute | solution.py:240
  88.6 1.8 %collective-permute-done.28.refs_2_ = bf16[96,1024]{1,0:T(8,128)(2,1)S(1)} collective-permute-done((bf16[96,1024]{1,0:T(8,128)(2,1)S(1)}, bf16[96,1024]{1,0:T(8,128)(2,1)S(1)}, u32[]{:S(2)}, u32[]{:S(2)}) %collective-permute-start.28) | collective-permute-done | bytes 196640 | tf_op jit(solution)/shard_map/ppermute | solution.py:240
  90.4 0.9 %shard_map.49 = f32[80,1024]{1,0:T(8,128)} custom-call(f32[80,1024]{1,0:T(8,128)S(1)} %get-tuple-element.61.own_ref, bf16[80,1152]{1,0:T(8,128)(2,1)S(1)} %shard_map.28.refs_0_.packed_ref, f32[2,1024]{1,0:T(2,128)S(1)} %shard_map.47.sums_ref, bf16[96,1024]{1,0:T(8,128)(2,1)S(1)} %collective-permute-done.26.refs_0_, ...), custom_call_target="tpu_custom_call" | custom-call | tf_op jit(solution)/shard_map/pallas_call | solution.py:31
  (36 shorter events, 0.2 us)
Async XLA Ops:
  0.0 0.9 %copy-start = (bf16[80,1024]{1,0:T(8,128)(2,1)S(1)}, bf16[80,1024]{1,0:T(8,128)(2,1)}, u32[]{:S(2)}) copy-start(bf16[80,1024]{1,0:T(8,128)(2,1)} %clips_hbm.1) | copy-start | bytes 491524
  0.9 0.7 copy-start.1
  2.1 10.6 %collective-permute-start.4 = (bf16[80,1152]{1,0:T(8,128)(2,1)S(1)}, bf16[80,1152]{1,0:T(8,128)(2,1)S(1)}, u32[]{:S(2)}, u32[]{:S(2)}) collective-permute-start(bf16[80,1152]{1,0:T(8,128)(2,1)S(1)} %shard_map.28.refs_0_.packed_ref), channel_id=1, source_target_pairs={{0,196},{4,0},{64,4},{68,64},{128,68},{132,128},{192,132},{196,192... | collective-permute-start | bytes 552968 | tf_op jit(solution)/shard_map/ppermute | solution.py:228
  8.0 7.9 %collective-permute-start.3 = (bf16[80,1152]{1,0:T(8,128)(2,1)S(1)}, bf16[80,1152]{1,0:T(8,128)(2,1)S(1)}, u32[]{:S(2)}, u32[]{:S(2)}) collective-permute-start(bf16[80,1152]{1,0:T(8,128)(2,1)S(1)} %shard_map.28.refs_0_.packed_ref), channel_id=1, source_target_pairs={{0,4},{4,64},{64,68},{68,128},{128,132},{132,192},{192,196},{196,0... | collective-permute-start | bytes 552968 | tf_op jit(solution)/shard_map/ppermute | solution.py:228
  8.0 7.9 %collective-permute-start.2 = (bf16[80,1152]{1,0:T(8,128)(2,1)S(1)}, bf16[80,1152]{1,0:T(8,128)(2,1)S(1)}, u32[]{:S(2)}, u32[]{:S(2)}) collective-permute-start(bf16[80,1152]{1,0:T(8,128)(2,1)S(1)} %shard_map.28.refs_0_.packed_ref), channel_id=1, source_target_pairs={{0,2},{1,3},{2,0},{3,1},{8,40},{9,41},{10,42},{11,43},{16,18},{17,... | collective-permute-start | bytes 552968 | tf_op jit(solution)/shard_map/ppermute | solution.py:240
  9.4 7.6 %collective-permute-start.1 = (bf16[80,1152]{1,0:T(8,128)(2,1)S(1)}, bf16[80,1152]{1,0:T(8,128)(2,1)S(1)}, u32[]{:S(2)}, u32[]{:S(2)}) collective-permute-start(bf16[80,1152]{1,0:T(8,128)(2,1)S(1)} %shard_map.28.refs_0_.packed_ref), channel_id=1, source_target_pairs={{0,3},{1,0},{2,1},{3,2},{8,56},{9,57},{10,58},{11,59},{16,19},{17,... | collective-permute-start | bytes 552968 | tf_op jit(solution)/shard_map/ppermute | solution.py:240
  9.4 7.6 %collective-permute-start = (bf16[80,1152]{1,0:T(8,128)(2,1)S(1)}, bf16[80,1152]{1,0:T(8,128)(2,1)S(1)}, u32[]{:S(2)}, u32[]{:S(2)}) collective-permute-start(bf16[80,1152]{1,0:T(8,128)(2,1)S(1)} %shard_map.28.refs_0_.packed_ref), channel_id=1, source_target_pairs={{0,1},{1,2},{2,3},{3,0},{8,24},{9,25},{10,26},{11,27},{16,17},{17,... | collective-permute-start | bytes 552968 | tf_op jit(solution)/shard_map/ppermute | solution.py:240
  12.6 9.7 %collective-permute-start.10 = (bf16[80,1152]{1,0:T(8,128)(2,1)S(1)}, bf16[80,1152]{1,0:T(8,128)(2,1)S(1)}, u32[]{:S(2)}, u32[]{:S(2)}) collective-permute-start(bf16[80,1152]{1,0:T(8,128)(2,1)S(1)} %collective-permute-done.4.refs_5_.refs_4_), channel_id=1, source_target_pairs={{0,196},{4,0},{64,4},{68,64},{128,68},{132,128},{192,132},{196,192... | collective-permute-start | bytes 552968 | tf_op jit(solution)/shard_map/ppermute | solution.py:228
  15.9 9.7 %collective-permute-start.8 = (bf16[80,1152]{1,0:T(8,128)(2,1)S(1)}, bf16[80,1152]{1,0:T(8,128)(2,1)S(1)}, u32[]{:S(2)}, u32[]{:S(2)}) collective-permute-start(bf16[80,1152]{1,0:T(8,128)(2,1)S(1)} %collective-permute-done.3.refs_4_.refs_1_), channel_id=1, source_target_pairs={{0,4},{4,64},{64,68},{68,128},{128,132},{132,192},{192,196},{196,0... | collective-permute-start | bytes 552968 | tf_op jit(solution)/shard_map/ppermute | solution.py:228
  17.1 30.7 %collective-permute-start.7 = (bf16[320,1152]{1,0:T(8,128)(2,1)S(1)}, bf16[320,1152]{1,0:T(8,128)(2,1)S(1)}, u32[]{:S(2)}, u32[]{:S(2)}) collective-permute-start(bf16[320,1152]{1,0:T(8,128)(2,1)S(1)} %shard_map.29.refs_3_), channel_id=1, source_target_pairs={{0,32},{1,33},{2,34},{3,35},{8,10},{9,11},{10,8},{11,9},{16,48},{1... | collective-permute-start | bytes 2211848 | tf_op jit(solution)/shard_map/ppermute | solution.py:240
  20.4 27.4 %collective-permute-start.6 = (bf16[320,1152]{1,0:T(8,128)(2,1)S(1)}, bf16[320,1152]{1,0:T(8,128)(2,1)S(1)}, u32[]{:S(2)}, u32[]{:S(2)}) collective-permute-start(bf16[320,1152]{1,0:T(8,128)(2,1)S(1)} %shard_map.29.refs_3_), channel_id=1, source_target_pairs={{0,48},{1,49},{2,50},{3,51},{8,11},{9,8},{10,9},{11,10},{16,0},{17... | collective-permute-start | bytes 2211848 | tf_op jit(solution)/shard_map/ppermute | solution.py:240
  21.4 26.4 %collective-permute-start.5 = (bf16[320,1152]{1,0:T(8,128)(2,1)S(1)}, bf16[320,1152]{1,0:T(8,128)(2,1)S(1)}, u32[]{:S(2)}, u32[]{:S(2)}) collective-permute-start(bf16[320,1152]{1,0:T(8,128)(2,1)S(1)} %shard_map.29.refs_3_), channel_id=1, source_target_pairs={{0,16},{1,17},{2,18},{3,19},{8,9},{9,10},{10,11},{11,8},{16,32},{1... | collective-permute-start | bytes 2211848 | tf_op jit(solution)/shard_map/ppermute | solution.py:240
  22.4 6.3 %collective-permute-start.11 = (bf16[80,1152]{1,0:T(8,128)(2,1)S(1)}, bf16[80,1152]{1,0:T(8,128)(2,1)S(1)}, u32[]{:S(2)}, u32[]{:S(2)}) collective-permute-start(bf16[80,1152]{1,0:T(8,128)(2,1)S(1)} %collective-permute-done.10.refs_5_), channel_id=1, source_target_pairs={{0,196},{4,0},{64,4},{68,64},{128,68},{132,128},{192,132},{196,192... | collective-permute-start | bytes 552968 | tf_op jit(solution)/shard_map/ppermute | solution.py:228
  25.6 6.7 %collective-permute-start.9 = (bf16[80,1152]{1,0:T(8,128)(2,1)S(1)}, bf16[80,1152]{1,0:T(8,128)(2,1)S(1)}, u32[]{:S(2)}, u32[]{:S(2)}) collective-permute-start(bf16[80,1152]{1,0:T(8,128)(2,1)S(1)} %collective-permute-done.8.refs_2_), channel_id=1, source_target_pairs={{0,4},{4,64},{64,68},{68,128},{128,132},{132,192},{192,196},{196,0... | collective-permute-start | bytes 552968 | tf_op jit(solution)/shard_map/ppermute | solution.py:228
  32.5 15.4 %collective-permute-start.12 = (bf16[560,1152]{1,0:T(8,128)(2,1)S(1)}, bf16[560,1152]{1,0:T(8,128)(2,1)S(1)}, u32[]{:S(2)}, u32[]{:S(2)}) collective-permute-start(bf16[560,1152]{1,0:T(8,128)(2,1)S(1)} %shard_map.33.block_ref.refs_4_), channel_id=1, source_target_pairs={{0,8},{8,0},{1,9},{9,1},{2,10},{10,2},{3,11},{11,3},{4,12},{12,4},... | collective-permute-start | bytes 3870728 | tf_op jit(solution)/shard_map/ppermute | solution.py:228
  32.6 7.1 %collective-permute-start.13 = (bf16[80,1152]{1,0:T(8,128)(2,1)S(1)}, bf16[80,1152]{1,0:T(8,128)(2,1)S(1)}, u32[]{:S(2)}, u32[]{:S(2)}) collective-permute-start(bf16[80,1152]{1,0:T(8,128)(2,1)S(1)} %collective-permute-done.11.refs_6_), channel_id=1, source_target_pairs={{0,196},{4,0},{64,4},{68,64},{128,68},{132,128},{192,132},{196,192... | collective-permute-start | bytes 552968 | tf_op jit(solution)/shard_map/ppermute | solution.py:228
  39.6 8.0 %collective-permute-start.14 = (bf16[80,1152]{1,0:T(8,128)(2,1)S(1)}, bf16[80,1152]{1,0:T(8,128)(2,1)S(1)}, u32[]{:S(2)}, u32[]{:S(2)}) collective-permute-start(bf16[80,1152]{1,0:T(8,128)(2,1)S(1)} %collective-permute-done.9.refs_3_), channel_id=1, source_target_pairs={{0,12},{4,72},{64,76},{68,136},{128,140},{132,200},{192,204},{196,... | collective-permute-start | bytes 552968 | tf_op jit(solution)/shard_map/ppermute | solution.py:248
  53.9 15.2 %collective-permute-start.15 = (bf16[320,1024]{1,0:T(8,128)(2,1)S(1)}, bf16[320,1024]{1,0:T(8,128)(2,1)S(1)}, u32[]{:S(2)}, u32[]{:S(2)}) collective-permute-start(bf16[320,1024]{1,0:T(8,128)(2,1)S(1)} %shard_map.40.refs_3_), channel_id=1, source_target_pairs={{0,48},{1,49},{2,50},{3,51},{8,11},{9,8},{10,9},{11,10},{16,0},{17... | collective-permute-start | bytes 1966088 | tf_op jit(solution)/shard_map/ppermute | solution.py:240
  56.3 4.9 %collective-permute-start.18 = (f32[2,1024]{1,0:T(2,128)S(1)}, f32[2,1024]{1,0:T(2,128)S(1)}, u32[]{:S(2)}, u32[]{:S(2)}) collective-permute-start(f32[2,1024]{1,0:T(2,128)S(1)} %get-tuple-element.60.refs_0_), channel_id=1, source_target_pairs={{0,4},{4,64},{64,68},{68,128},{128,132},{132,192},{192,196},{196,0... | collective-permute-start | bytes 24584 | tf_op jit(solution)/shard_map/ppermute | solution.py:228
  56.3 4.9 %collective-permute-start.19 = (f32[2,1024]{1,0:T(2,128)S(1)}, f32[2,1024]{1,0:T(2,128)S(1)}, u32[]{:S(2)}, u32[]{:S(2)}) collective-permute-start(f32[2,1024]{1,0:T(2,128)S(1)} %get-tuple-element.60.refs_0_), channel_id=1, source_target_pairs={{0,196},{4,0},{64,4},{68,64},{128,68},{132,128},{192,132},{196,192... | collective-permute-start | bytes 24584 | tf_op jit(solution)/shard_map/ppermute | solution.py:228
  60.6 19.0 %collective-permute-start.16 = (bf16[320,1024]{1,0:T(8,128)(2,1)S(1)}, bf16[320,1024]{1,0:T(8,128)(2,1)S(1)}, u32[]{:S(2)}, u32[]{:S(2)}) collective-permute-start(bf16[320,1024]{1,0:T(8,128)(2,1)S(1)} %shard_map.41.refs_4_), channel_id=1, source_target_pairs={{0,16},{1,17},{2,18},{3,19},{8,9},{9,10},{10,11},{11,8},{16,32},{1... | collective-permute-start | bytes 1966088 | tf_op jit(solution)/shard_map/ppermute | solution.py:240
  61.1 6.1 %collective-permute-start.21 = (f32[2,1024]{1,0:T(2,128)S(1)}, f32[2,1024]{1,0:T(2,128)S(1)}, u32[]{:S(2)}, u32[]{:S(2)}) collective-permute-start(f32[2,1024]{1,0:T(2,128)S(1)} %shard_map.44), channel_id=1, source_target_pairs={{0,132},{4,192},{64,196},{68,0},{128,4},{132,64},{192,68},{196,128... | collective-permute-start | bytes 24584 | tf_op jit(solution)/shard_map/ppermute | solution.py:228
  61.2 6.7 %collective-permute-start.20 = (f32[2,1024]{1,0:T(2,128)S(1)}, f32[2,1024]{1,0:T(2,128)S(1)}, u32[]{:S(2)}, u32[]{:S(2)}) collective-permute-start(f32[2,1024]{1,0:T(2,128)S(1)} %shard_map.43.refs_0_), channel_id=1, source_target_pairs={{0,68},{4,128},{64,132},{68,192},{128,196},{132,0},{192,4},{196,64... | collective-permute-start | bytes 24584 | tf_op jit(solution)/shard_map/ppermute | solution.py:228
  66.0 13.6 %collective-permute-start.17 = (bf16[320,1024]{1,0:T(8,128)(2,1)S(1)}, bf16[320,1024]{1,0:T(8,128)(2,1)S(1)}, u32[]{:S(2)}, u32[]{:S(2)}) collective-permute-start(bf16[320,1024]{1,0:T(8,128)(2,1)S(1)} %shard_map.42.refs_3_), channel_id=1, source_target_pairs={{0,32},{1,33},{2,34},{3,35},{8,10},{9,11},{10,8},{11,9},{16,48},{1... | collective-permute-start | bytes 1966088 | tf_op jit(solution)/shard_map/ppermute | solution.py:240
  67.9 1.2 %collective-permute-start.22 = (f32[2,1024]{1,0:T(2,128)S(1)}, f32[2,1024]{1,0:T(2,128)S(1)}, u32[]{:S(2)}, u32[]{:S(2)}) collective-permute-start(f32[2,1024]{1,0:T(2,128)S(1)} %shard_map.45.refs_0_), channel_id=1, source_target_pairs={{0,8},{8,0},{1,9},{9,1},{2,10},{10,2},{3,11},{11,3},{4,12},{12,4},... | collective-permute-start | bytes 24584 | tf_op jit(solution)/shard_map/ppermute | solution.py:228
  69.1 10.5 %collective-permute-start.25 = (f32[2,1024]{1,0:T(2,128)S(1)}, f32[2,1024]{1,0:T(2,128)S(1)}, u32[]{:S(2)}, u32[]{:S(2)}) collective-permute-start(f32[2,1024]{1,0:T(2,128)S(1)} %shard_map.46.refs_0_), channel_id=1, source_target_pairs={{0,32},{1,33},{2,34},{3,35},{8,10},{9,11},{10,8},{11,9},{16,48},{1... | collective-permute-start | bytes 24584 | tf_op jit(solution)/shard_map/ppermute | solution.py:240
  71.1 8.4 %collective-permute-start.24 = (f32[2,1024]{1,0:T(2,128)S(1)}, f32[2,1024]{1,0:T(2,128)S(1)}, u32[]{:S(2)}, u32[]{:S(2)}) collective-permute-start(f32[2,1024]{1,0:T(2,128)S(1)} %shard_map.46.refs_0_), channel_id=1, source_target_pairs={{0,48},{1,49},{2,50},{3,51},{8,11},{9,8},{10,9},{11,10},{16,0},{17... | collective-permute-start | bytes 24584 | tf_op jit(solution)/shard_map/ppermute | solution.py:240
  73.9 5.8 %collective-permute-start.23 = (f32[2,1024]{1,0:T(2,128)S(1)}, f32[2,1024]{1,0:T(2,128)S(1)}, u32[]{:S(2)}, u32[]{:S(2)}) collective-permute-start(f32[2,1024]{1,0:T(2,128)S(1)} %shard_map.46.refs_0_), channel_id=1, source_target_pairs={{0,16},{1,17},{2,18},{3,19},{8,9},{9,10},{10,11},{11,8},{16,32},{1... | collective-permute-start | bytes 24584 | tf_op jit(solution)/shard_map/ppermute | solution.py:240
  79.9 7.0 %collective-permute-start.26 = (bf16[96,1024]{1,0:T(8,128)(2,1)S(1)}, bf16[96,1024]{1,0:T(8,128)(2,1)S(1)}, u32[]{:S(2)}, u32[]{:S(2)}) collective-permute-start(bf16[96,1024]{1,0:T(8,128)(2,1)S(1)} %get-tuple-element.62), channel_id=1, source_target_pairs={{0,3},{1,0},{2,1},{3,2},{8,56},{9,57},{10,58},{11,59},{16,19},{17,... | collective-permute-start | bytes 589832 | tf_op jit(solution)/shard_map/ppermute | solution.py:240
  80.8 7.7 %collective-permute-start.27 = (bf16[96,1024]{1,0:T(8,128)(2,1)S(1)}, bf16[96,1024]{1,0:T(8,128)(2,1)S(1)}, u32[]{:S(2)}, u32[]{:S(2)}) collective-permute-start(bf16[96,1024]{1,0:T(8,128)(2,1)S(1)} %get-tuple-element.63), channel_id=1, source_target_pairs={{0,1},{1,2},{2,3},{3,0},{8,24},{9,25},{10,26},{11,27},{16,17},{17,... | collective-permute-start | bytes 589832 | tf_op jit(solution)/shard_map/ppermute | solution.py:240
  83.3 7.2 %collective-permute-start.28 = (bf16[96,1024]{1,0:T(8,128)(2,1)S(1)}, bf16[96,1024]{1,0:T(8,128)(2,1)S(1)}, u32[]{:S(2)}, u32[]{:S(2)}) collective-permute-start(bf16[96,1024]{1,0:T(8,128)(2,1)S(1)} %get-tuple-element.64), channel_id=1, source_target_pairs={{0,2},{1,3},{2,0},{3,1},{8,40},{9,41},{10,42},{11,43},{16,18},{17,... | collective-permute-start | bytes 589832 | tf_op jit(solution)/shard_map/ppermute | solution.py:240
